TPU v7x, 512 devices: a whole 4x8x8 slice. The times are simulated.
512 devices in a mesh: seq: 64 (over y, x, core), chan: 8 (over z).
Axes of the slice: x: 4, y: 8, z: 8, core: 2. Of those that a mesh axis runs over, the one named last changes fastest.
Arguments:
- streams: bfloat16 [3, 16384, 8192], P(None, 'seq', 'chan'), may hold values from -6 to 6
- short_filter: float32 [3, 3, 8192], P(None, None, 'chan'), may hold values from -3 to 3
- pole_rates: float32 [16, 8192], P(None, 'chan'), may hold values from 6.1035157e-06 to 0.03
- residues: float32 [16, 8192], P(None, 'chan'), may hold values from -3 to 3
- direct: float32 [8192], P('chan'), may hold values from -3 to 3
- doc_lengths: int32 [4], replicated, may hold values from 1 to 8192, 16384 in all
- targets: int32 [16384], P('seq'), may hold values from 0 to 511
- unembed: bfloat16 [8192, 512], P('chan'), may hold values from -0.7 to 0.7
Outputs:
- gated_out: bfloat16 [16384, 8192], P('seq', 'chan')
- token_loss: float32 [16384], P('seq')
All inputs are finite; a program needn't handle non-finite values.
Results may differ from a plain program's by a relative error of at most 0.012.
Values may be sent and summed in bfloat16 or wider, within the bound.
No kernel may reach another device: no remote copies, remote signals or barrier semaphores. Data moves between devices by JAX's collectives and lax.ppermute only.
A program may use at most 64 MiB of HBM per device.

v0:
```python
import jax
import jax.numpy as jnp
from jax import lax
from jax.sharding import PartitionSpec as P


def shifted(block, axis, distance):
    devices = range(lax.axis_size(axis))
    route = [(i - distance, i) for i in devices if i - distance in devices]
    return lax.ppermute(block, axis, route)


def local(streams, short_filter, pole_rates, residues, direct, doc_lengths, targets, unembed):
    block_len = streams.shape[1]
    chans = streams.shape[2]
    pole_count = pole_rates.shape[0]
    group_size = 4
    group_count = pole_count // group_size
    block_id = lax.axis_index("seq")
    first_pos = block_id * block_len
    local_ids = jnp.arange(block_len, dtype=jnp.int32)
    local_float = local_ids.astype(jnp.float32)
    position = first_pos + local_ids
    doc_first = jnp.cumsum(doc_lengths) - doc_lengths
    chosen = jnp.where(doc_first[None, :] <= position[:, None], doc_first[None, :], 0)
    doc_start = jnp.max(chosen, axis=1)
    edge_rows = shifted(streams[:, block_len - 2 :, :], "seq", 1)
    extended = jnp.concatenate([edge_rows, streams], axis=1).astype(jnp.float32)
    filtered = short_filter[:, 0, None, :] * extended[:, 2:, :]
    for shift_by in range(1, 3):
        in_doc = (position - shift_by >= doc_start).astype(jnp.float32)
        window_rows = extended[:, 2 - shift_by : 2 - shift_by + block_len, :]
        filtered = (
            filtered + short_filter[:, shift_by, None, :] * window_rows * in_doc[None, :, None]
        )
    q_stream = filtered[0]
    driver = filtered[1] * filtered[2]
    rel_start = doc_start - first_pos
    same_doc = (
        (local_ids[None, :] <= local_ids[:, None]) & (local_ids[None, :] >= rel_start[:, None])
    ).astype(jnp.float32)
    rate_groups = pole_rates.reshape(group_count, group_size, chans)
    residue_groups = residues.reshape(group_count, group_size, chans)

    def block_states(members):
        rate_g, residue_g = members
        rising = jnp.exp(rate_g[:, None, :] * local_float[None, :, None])
        weighted = rising * (1.0 - jnp.exp(-rate_g))[:, None, :] * driver[None, :, :]
        summed = jnp.einsum("ts,psc->ptc", same_doc, weighted, precision=lax.Precision.HIGHEST)
        states_g = summed * jnp.exp(-rate_g[:, None, :] * local_float[None, :, None])
        return (jnp.sum(residue_g[:, None, :] * states_g, axis=0), states_g[:, block_len - 1, :])

    partial_out, end_groups = lax.map(block_states, (rate_groups, residue_groups))
    long_out = jnp.sum(partial_out, axis=0)
    end_states = end_groups.reshape(pole_count, chans)
    keep_block = (doc_start[block_len - 1] < first_pos).astype(jnp.float32)
    transfer = jnp.exp(-pole_rates * block_len) * keep_block

    def relay_step(turn, arriving):
        return shifted(transfer * arriving + end_states, "seq", 1)

    incoming = lax.fori_loop(0, lax.axis_size("seq") - 1, relay_step, jnp.zeros_like(end_states))
    carried_in = (doc_start < first_pos).astype(jnp.float32)
    incoming_groups = incoming.reshape(group_count, group_size, chans)
    for group_id in range(group_count):
        weight_in = residue_groups[group_id] * incoming_groups[group_id]
        fading = jnp.exp(-rate_groups[group_id][:, None, :] * (local_float + 1.0)[None, :, None])
        long_out = long_out + carried_in[:, None] * jnp.sum(weight_in[:, None, :] * fading, axis=0)
    gated_out = (q_stream * (long_out + direct[None, :] * driver)).astype(jnp.bfloat16)
    partial_logits = jnp.dot(gated_out, unembed, preferred_element_type=jnp.float32)
    vocab_size = unembed.shape[1]
    logits = lax.psum(partial_logits.astype(jnp.bfloat16), "chan").astype(jnp.float32)
    peak = jnp.max(logits, axis=1)
    exp_total = jnp.sum(jnp.exp(logits - peak[:, None]), axis=1)
    vocab_ids = jnp.arange(vocab_size, dtype=jnp.int32)
    picked = jnp.sum(jnp.where(targets[:, None] == vocab_ids[None, :], logits, 0.0), axis=1)
    token_loss = peak + jnp.log(exp_total) - picked
    return (gated_out, token_loss)


def solution(mesh):
    in_specs = (
        P(None, "seq", "chan"),
        P(None, None, "chan"),
        P(None, "chan"),
        P(None, "chan"),
        P("chan"),
        P(),
        P("seq"),
        P("chan", None),
    )
    out_specs = (P("seq", "chan"), P("seq"))
    return jax.shard_map(local, mesh=mesh, in_specs=in_specs, out_specs=out_specs, check_vma=False)
```

profile of v0, /device:TPU:2, one launch (start us, length us, event | category | flops | bytes accessed | tf_op | source)
XLA Modules:
  0.0 716.6 jit_solution(8788606478191993373)
XLA Ops:
  22.3 32.7 %while.25 = (s32[]{:T(128)}, f32[4,256,1024]{2,1,0:T(8,128)}, f32[4,4,1024]{2,1,0:T(4,128)S(1)}, f32[4,4,1024]{2,1,0:T(4,128)S(1)}, f32[4,4,1024]{2,1,0:T(4,128)...) while((s32[]{:T(128)}, f32[4,256,1024]{2,1,0:T(8,128)}, ...), condition=%wide.region_4.5_spmd.clone.clone, body=%wide.region_2.4_spmd.clone.clone.sunk | while | flops 3228578048 | bytes 8637549 | solution.py:53
  22.6 6.9 multiply_reduce_fusion.6
  30.7 6.9 multiply_reduce_fusion.6
  38.8 6.9 multiply_reduce_fusion.6
  46.9 6.9 multiply_reduce_fusion.6
  55.0 462.2 %while.24 = (s32[]{:T(128)}, f32[16,1024]{1,0:T(8,128)S(1)}, f32[16,1024]{1,0:T(8,128)S(1)}, f32[16,1024]{1,0:T(8,128)S(1)}, s32[]{:T(128)}) while((s32[]{:T(128)}, f32[16,1024]{1,0:T(8,128)S(1)}, f32[16,1024]{1,0:T(8,128)S(1)}, f32[16,1024]{1,0:T(8,128)S(1)}, s32[]{:T(128)}) %tuple.65), condition=%wide.region_7.8_spmd, body=%wide.region_6.7_spmd.sunk | while | flops 32770 | bytes 524389 | solution.py:62
  124.0 6.8 collective-permute-start
  131.7 6.8 collective-permute-start
  139.4 6.8 collective-permute-start
  147.1 6.8 collective-permute-start
  154.8 6.8 collective-permute-start
  162.5 6.8 collective-permute-start
  170.2 6.8 collective-permute-start
  178.0 6.8 collective-permute-start
  185.7 6.8 collective-permute-start
  193.4 6.8 collective-permute-start
  201.1 6.8 collective-permute-start
  208.8 6.8 collective-permute-start
  216.5 6.8 collective-permute-start
  224.2 6.8 collective-permute-start
  231.9 6.8 collective-permute-start
  239.6 6.8 collective-permute-start
  247.4 6.8 collective-permute-start
  255.1 6.8 collective-permute-start
  262.8 6.8 collective-permute-start
  270.5 6.8 collective-permute-start
  278.2 6.8 collective-permute-start
  285.9 6.8 collective-permute-start
  293.6 6.8 collective-permute-start
  301.3 6.8 collective-permute-start
  309.0 6.8 collective-permute-start
  316.8 6.8 collective-permute-start
  324.5 6.8 collective-permute-start
  332.2 6.8 collective-permute-start
  339.9 6.8 collective-permute-start
  347.6 6.8 collective-permute-start
  355.3 6.8 collective-permute-start
  363.0 6.8 collective-permute-start
  370.7 6.8 collective-permute-start
  378.4 6.8 collective-permute-start
  386.2 6.8 collective-permute-start
  393.9 6.8 collective-permute-start
  401.6 6.8 collective-permute-start
  409.3 6.8 collective-permute-start
  417.0 6.8 collective-permute-start
  424.7 6.8 collective-permute-start
  455.6 6.8 collective-permute-start
  525.9 180.9 %all-reduce.2.cloned.1.call-done = bf16[256,512]{1,0:T(8,128)(2,1)} async-done(((bf16[256,512]{1,0:T(8,128)(2,1)}), bf16[256,512]{1,0:T(8,128)(2,1)}) %all-reduce.2.cloned.1.call-update) | async-done | bytes 262160 | tf_op jit(solution)/shard_map/psum | solution.py:72
  (226 shorter events, 212.6 us)
Async XLA Ops:
  7.2 699.6 %all-reduce.2.cloned.1.call-start = ((), (), s32[]{:S(2)}) async-start(), calls=%async_computation | async-start | bytes 524288 | tf_op jit(solution)/shard_map/psum | solution.py:72
  8.1 9.2 %collective-permute-start.1 = (bf16[3,2,1024]{2,1,0:T(2,128)(2,1)S(1)}, bf16[3,2,1024]{2,1,0:T(2,128)(2,1)S(1)}, u32[]{:S(2)}, u32[]{:S(2)}) collective-permute-start(bf16[3,2,1024]{2,1,0:T(2,128)(2,1)S(1)} %slice.85), channel_id=1, source_target_pairs={{0,8},{8,16},{16,24},{24,32},{32,40},{40,48},{48,56},{56,64},{64,7... | collective-permute-start | bytes 36872 | tf_op jit(solution)/shard_map/ppermute | solution.py:10
  124.0 7.7 %collective-permute-start = (f32[16,1024]{1,0:T(8,128)S(1)}, f32[16,1024]{1,0:T(8,128)S(1)}, u32[]{:S(2)}, u32[]{:S(2)}) collective-permute-start(f32[16,1024]{1,0:T(8,128)S(1)} %multiply_add_fusion.2), channel_id=1, source_target_pairs={{0,8},{8,16},{16,24},{24,32},{32,40},{40,48},{48,56},{56,64},{64,7... | collective-permute-start | bytes 196616 | tf_op jit(solution)/shard_map/while/body/eval_jaxpr/ppermute | solution.py:10
  131.7 7.7 %collective-permute-start = (f32[16,1024]{1,0:T(8,128)S(1)}, f32[16,1024]{1,0:T(8,128)S(1)}, u32[]{:S(2)}, u32[]{:S(2)}) collective-permute-start(f32[16,1024]{1,0:T(8,128)S(1)} %multiply_add_fusion.2), channel_id=1, source_target_pairs={{0,8},{8,16},{16,24},{24,32},{32,40},{40,48},{48,56},{56,64},{64,7... | collective-permute-start | bytes 196616 | tf_op jit(solution)/shard_map/while/body/eval_jaxpr/ppermute | solution.py:10
  139.4 7.7 %collective-permute-start = (f32[16,1024]{1,0:T(8,128)S(1)}, f32[16,1024]{1,0:T(8,128)S(1)}, u32[]{:S(2)}, u32[]{:S(2)}) collective-permute-start(f32[16,1024]{1,0:T(8,128)S(1)} %multiply_add_fusion.2), channel_id=1, source_target_pairs={{0,8},{8,16},{16,24},{24,32},{32,40},{40,48},{48,56},{56,64},{64,7... | collective-permute-start | bytes 196616 | tf_op jit(solution)/shard_map/while/body/eval_jaxpr/ppermute | solution.py:10
  147.1 7.7 %collective-permute-start = (f32[16,1024]{1,0:T(8,128)S(1)}, f32[16,1024]{1,0:T(8,128)S(1)}, u32[]{:S(2)}, u32[]{:S(2)}) collective-permute-start(f32[16,1024]{1,0:T(8,128)S(1)} %multiply_add_fusion.2), channel_id=1, source_target_pairs={{0,8},{8,16},{16,24},{24,32},{32,40},{40,48},{48,56},{56,64},{64,7... | collective-permute-start | bytes 196616 | tf_op jit(solution)/shard_map/while/body/eval_jaxpr/ppermute | solution.py:10
  154.8 7.7 %collective-permute-start = (f32[16,1024]{1,0:T(8,128)S(1)}, f32[16,1024]{1,0:T(8,128)S(1)}, u32[]{:S(2)}, u32[]{:S(2)}) collective-permute-start(f32[16,1024]{1,0:T(8,128)S(1)} %multiply_add_fusion.2), channel_id=1, source_target_pairs={{0,8},{8,16},{16,24},{24,32},{32,40},{40,48},{48,56},{56,64},{64,7... | collective-permute-start | bytes 196616 | tf_op jit(solution)/shard_map/while/body/eval_jaxpr/ppermute | solution.py:10
  162.5 7.7 %collective-permute-start = (f32[16,1024]{1,0:T(8,128)S(1)}, f32[16,1024]{1,0:T(8,128)S(1)}, u32[]{:S(2)}, u32[]{:S(2)}) collective-permute-start(f32[16,1024]{1,0:T(8,128)S(1)} %multiply_add_fusion.2), channel_id=1, source_target_pairs={{0,8},{8,16},{16,24},{24,32},{32,40},{40,48},{48,56},{56,64},{64,7... | collective-permute-start | bytes 196616 | tf_op jit(solution)/shard_map/while/body/eval_jaxpr/ppermute | solution.py:10
  170.2 7.7 %collective-permute-start = (f32[16,1024]{1,0:T(8,128)S(1)}, f32[16,1024]{1,0:T(8,128)S(1)}, u32[]{:S(2)}, u32[]{:S(2)}) collective-permute-start(f32[16,1024]{1,0:T(8,128)S(1)} %multiply_add_fusion.2), channel_id=1, source_target_pairs={{0,8},{8,16},{16,24},{24,32},{32,40},{40,48},{48,56},{56,64},{64,7... | collective-permute-start | bytes 196616 | tf_op jit(solution)/shard_map/while/body/eval_jaxpr/ppermute | solution.py:10
  178.0 7.7 %collective-permute-start = (f32[16,1024]{1,0:T(8,128)S(1)}, f32[16,1024]{1,0:T(8,128)S(1)}, u32[]{:S(2)}, u32[]{:S(2)}) collective-permute-start(f32[16,1024]{1,0:T(8,128)S(1)} %multiply_add_fusion.2), channel_id=1, source_target_pairs={{0,8},{8,16},{16,24},{24,32},{32,40},{40,48},{48,56},{56,64},{64,7... | collective-permute-start | bytes 196616 | tf_op jit(solution)/shard_map/while/body/eval_jaxpr/ppermute | solution.py:10
  185.7 7.7 %collective-permute-start = (f32[16,1024]{1,0:T(8,128)S(1)}, f32[16,1024]{1,0:T(8,128)S(1)}, u32[]{:S(2)}, u32[]{:S(2)}) collective-permute-start(f32[16,1024]{1,0:T(8,128)S(1)} %multiply_add_fusion.2), channel_id=1, source_target_pairs={{0,8},{8,16},{16,24},{24,32},{32,40},{40,48},{48,56},{56,64},{64,7... | collective-permute-start | bytes 196616 | tf_op jit(solution)/shard_map/while/body/eval_jaxpr/ppermute | solution.py:10
  193.4 7.7 %collective-permute-start = (f32[16,1024]{1,0:T(8,128)S(1)}, f32[16,1024]{1,0:T(8,128)S(1)}, u32[]{:S(2)}, u32[]{:S(2)}) collective-permute-start(f32[16,1024]{1,0:T(8,128)S(1)} %multiply_add_fusion.2), channel_id=1, source_target_pairs={{0,8},{8,16},{16,24},{24,32},{32,40},{40,48},{48,56},{56,64},{64,7... | collective-permute-start | bytes 196616 | tf_op jit(solution)/shard_map/while/body/eval_jaxpr/ppermute | solution.py:10
  201.1 7.7 %collective-permute-start = (f32[16,1024]{1,0:T(8,128)S(1)}, f32[16,1024]{1,0:T(8,128)S(1)}, u32[]{:S(2)}, u32[]{:S(2)}) collective-permute-start(f32[16,1024]{1,0:T(8,128)S(1)} %multiply_add_fusion.2), channel_id=1, source_target_pairs={{0,8},{8,16},{16,24},{24,32},{32,40},{40,48},{48,56},{56,64},{64,7... | collective-permute-start | bytes 196616 | tf_op jit(solution)/shard_map/while/body/eval_jaxpr/ppermute | solution.py:10
  208.8 7.7 %collective-permute-start = (f32[16,1024]{1,0:T(8,128)S(1)}, f32[16,1024]{1,0:T(8,128)S(1)}, u32[]{:S(2)}, u32[]{:S(2)}) collective-permute-start(f32[16,1024]{1,0:T(8,128)S(1)} %multiply_add_fusion.2), channel_id=1, source_target_pairs={{0,8},{8,16},{16,24},{24,32},{32,40},{40,48},{48,56},{56,64},{64,7... | collective-permute-start | bytes 196616 | tf_op jit(solution)/shard_map/while/body/eval_jaxpr/ppermute | solution.py:10
  216.5 7.7 %collective-permute-start = (f32[16,1024]{1,0:T(8,128)S(1)}, f32[16,1024]{1,0:T(8,128)S(1)}, u32[]{:S(2)}, u32[]{:S(2)}) collective-permute-start(f32[16,1024]{1,0:T(8,128)S(1)} %multiply_add_fusion.2), channel_id=1, source_target_pairs={{0,8},{8,16},{16,24},{24,32},{32,40},{40,48},{48,56},{56,64},{64,7... | collective-permute-start | bytes 196616 | tf_op jit(solution)/shard_map/while/body/eval_jaxpr/ppermute | solution.py:10
  224.2 7.7 %collective-permute-start = (f32[16,1024]{1,0:T(8,128)S(1)}, f32[16,1024]{1,0:T(8,128)S(1)}, u32[]{:S(2)}, u32[]{:S(2)}) collective-permute-start(f32[16,1024]{1,0:T(8,128)S(1)} %multiply_add_fusion.2), channel_id=1, source_target_pairs={{0,8},{8,16},{16,24},{24,32},{32,40},{40,48},{48,56},{56,64},{64,7... | collective-permute-start | bytes 196616 | tf_op jit(solution)/shard_map/while/body/eval_jaxpr/ppermute | solution.py:10
  231.9 7.7 %collective-permute-start = (f32[16,1024]{1,0:T(8,128)S(1)}, f32[16,1024]{1,0:T(8,128)S(1)}, u32[]{:S(2)}, u32[]{:S(2)}) collective-permute-start(f32[16,1024]{1,0:T(8,128)S(1)} %multiply_add_fusion.2), channel_id=1, source_target_pairs={{0,8},{8,16},{16,24},{24,32},{32,40},{40,48},{48,56},{56,64},{64,7... | collective-permute-start | bytes 196616 | tf_op jit(solution)/shard_map/while/body/eval_jaxpr/ppermute | solution.py:10
  239.6 7.7 %collective-permute-start = (f32[16,1024]{1,0:T(8,128)S(1)}, f32[16,1024]{1,0:T(8,128)S(1)}, u32[]{:S(2)}, u32[]{:S(2)}) collective-permute-start(f32[16,1024]{1,0:T(8,128)S(1)} %multiply_add_fusion.2), channel_id=1, source_target_pairs={{0,8},{8,16},{16,24},{24,32},{32,40},{40,48},{48,56},{56,64},{64,7... | collective-permute-start | bytes 196616 | tf_op jit(solution)/shard_map/while/body/eval_jaxpr/ppermute | solution.py:10
  247.4 7.7 %collective-permute-start = (f32[16,1024]{1,0:T(8,128)S(1)}, f32[16,1024]{1,0:T(8,128)S(1)}, u32[]{:S(2)}, u32[]{:S(2)}) collective-permute-start(f32[16,1024]{1,0:T(8,128)S(1)} %multiply_add_fusion.2), channel_id=1, source_target_pairs={{0,8},{8,16},{16,24},{24,32},{32,40},{40,48},{48,56},{56,64},{64,7... | collective-permute-start | bytes 196616 | tf_op jit(solution)/shard_map/while/body/eval_jaxpr/ppermute | solution.py:10
  255.1 7.7 %collective-permute-start = (f32[16,1024]{1,0:T(8,128)S(1)}, f32[16,1024]{1,0:T(8,128)S(1)}, u32[]{:S(2)}, u32[]{:S(2)}) collective-permute-start(f32[16,1024]{1,0:T(8,128)S(1)} %multiply_add_fusion.2), channel_id=1, source_target_pairs={{0,8},{8,16},{16,24},{24,32},{32,40},{40,48},{48,56},{56,64},{64,7... | collective-permute-start | bytes 196616 | tf_op jit(solution)/shard_map/while/body/eval_jaxpr/ppermute | solution.py:10
  262.8 7.7 %collective-permute-start = (f32[16,1024]{1,0:T(8,128)S(1)}, f32[16,1024]{1,0:T(8,128)S(1)}, u32[]{:S(2)}, u32[]{:S(2)}) collective-permute-start(f32[16,1024]{1,0:T(8,128)S(1)} %multiply_add_fusion.2), channel_id=1, source_target_pairs={{0,8},{8,16},{16,24},{24,32},{32,40},{40,48},{48,56},{56,64},{64,7... | collective-permute-start | bytes 196616 | tf_op jit(solution)/shard_map/while/body/eval_jaxpr/ppermute | solution.py:10
  270.5 7.7 %collective-permute-start = (f32[16,1024]{1,0:T(8,128)S(1)}, f32[16,1024]{1,0:T(8,128)S(1)}, u32[]{:S(2)}, u32[]{:S(2)}) collective-permute-start(f32[16,1024]{1,0:T(8,128)S(1)} %multiply_add_fusion.2), channel_id=1, source_target_pairs={{0,8},{8,16},{16,24},{24,32},{32,40},{40,48},{48,56},{56,64},{64,7... | collective-permute-start | bytes 196616 | tf_op jit(solution)/shard_map/while/body/eval_jaxpr/ppermute | solution.py:10
  278.2 7.7 %collective-permute-start = (f32[16,1024]{1,0:T(8,128)S(1)}, f32[16,1024]{1,0:T(8,128)S(1)}, u32[]{:S(2)}, u32[]{:S(2)}) collective-permute-start(f32[16,1024]{1,0:T(8,128)S(1)} %multiply_add_fusion.2), channel_id=1, source_target_pairs={{0,8},{8,16},{16,24},{24,32},{32,40},{40,48},{48,56},{56,64},{64,7... | collective-permute-start | bytes 196616 | tf_op jit(solution)/shard_map/while/body/eval_jaxpr/ppermute | solution.py:10
  293.6 7.7 %collective-permute-start = (f32[16,1024]{1,0:T(8,128)S(1)}, f32[16,1024]{1,0:T(8,128)S(1)}, u32[]{:S(2)}, u32[]{:S(2)}) collective-permute-start(f32[16,1024]{1,0:T(8,128)S(1)} %multiply_add_fusion.2), channel_id=1, source_target_pairs={{0,8},{8,16},{16,24},{24,32},{32,40},{40,48},{48,56},{56,64},{64,7... | collective-permute-start | bytes 196616 | tf_op jit(solution)/shard_map/while/body/eval_jaxpr/ppermute | solution.py:10
  301.3 7.7 %collective-permute-start = (f32[16,1024]{1,0:T(8,128)S(1)}, f32[16,1024]{1,0:T(8,128)S(1)}, u32[]{:S(2)}, u32[]{:S(2)}) collective-permute-start(f32[16,1024]{1,0:T(8,128)S(1)} %multiply_add_fusion.2), channel_id=1, source_target_pairs={{0,8},{8,16},{16,24},{24,32},{32,40},{40,48},{48,56},{56,64},{64,7... | collective-permute-start | bytes 196616 | tf_op jit(solution)/shard_map/while/body/eval_jaxpr/ppermute | solution.py:10
  309.0 7.7 %collective-permute-start = (f32[16,1024]{1,0:T(8,128)S(1)}, f32[16,1024]{1,0:T(8,128)S(1)}, u32[]{:S(2)}, u32[]{:S(2)}) collective-permute-start(f32[16,1024]{1,0:T(8,128)S(1)} %multiply_add_fusion.2), channel_id=1, source_target_pairs={{0,8},{8,16},{16,24},{24,32},{32,40},{40,48},{48,56},{56,64},{64,7... | collective-permute-start | bytes 196616 | tf_op jit(solution)/shard_map/while/body/eval_jaxpr/ppermute | solution.py:10
  316.8 7.7 %collective-permute-start = (f32[16,1024]{1,0:T(8,128)S(1)}, f32[16,1024]{1,0:T(8,128)S(1)}, u32[]{:S(2)}, u32[]{:S(2)}) collective-permute-start(f32[16,1024]{1,0:T(8,128)S(1)} %multiply_add_fusion.2), channel_id=1, source_target_pairs={{0,8},{8,16},{16,24},{24,32},{32,40},{40,48},{48,56},{56,64},{64,7... | collective-permute-start | bytes 196616 | tf_op jit(solution)/shard_map/while/body/eval_jaxpr/ppermute | solution.py:10
  324.5 7.7 %collective-permute-start = (f32[16,1024]{1,0:T(8,128)S(1)}, f32[16,1024]{1,0:T(8,128)S(1)}, u32[]{:S(2)}, u32[]{:S(2)}) collective-permute-start(f32[16,1024]{1,0:T(8,128)S(1)} %multiply_add_fusion.2), channel_id=1, source_target_pairs={{0,8},{8,16},{16,24},{24,32},{32,40},{40,48},{48,56},{56,64},{64,7... | collective-permute-start | bytes 196616 | tf_op jit(solution)/shard_map/while/body/eval_jaxpr/ppermute | solution.py:10
  332.2 7.7 %collective-permute-start = (f32[16,1024]{1,0:T(8,128)S(1)}, f32[16,1024]{1,0:T(8,128)S(1)}, u32[]{:S(2)}, u32[]{:S(2)}) collective-permute-start(f32[16,1024]{1,0:T(8,128)S(1)} %multiply_add_fusion.2), channel_id=1, source_target_pairs={{0,8},{8,16},{16,24},{24,32},{32,40},{40,48},{48,56},{56,64},{64,7... | collective-permute-start | bytes 196616 | tf_op jit(solution)/shard_map/while/body/eval_jaxpr/ppermute | solution.py:10
  339.9 7.7 %collective-permute-start = (f32[16,1024]{1,0:T(8,128)S(1)}, f32[16,1024]{1,0:T(8,128)S(1)}, u32[]{:S(2)}, u32[]{:S(2)}) collective-permute-start(f32[16,1024]{1,0:T(8,128)S(1)} %multiply_add_fusion.2), channel_id=1, source_target_pairs={{0,8},{8,16},{16,24},{24,32},{32,40},{40,48},{48,56},{56,64},{64,7... | collective-permute-start | bytes 196616 | tf_op jit(solution)/shard_map/while/body/eval_jaxpr/ppermute | solution.py:10
  355.3 7.7 %collective-permute-start = (f32[16,1024]{1,0:T(8,128)S(1)}, f32[16,1024]{1,0:T(8,128)S(1)}, u32[]{:S(2)}, u32[]{:S(2)}) collective-permute-start(f32[16,1024]{1,0:T(8,128)S(1)} %multiply_add_fusion.2), channel_id=1, source_target_pairs={{0,8},{8,16},{16,24},{24,32},{32,40},{40,48},{48,56},{56,64},{64,7... | collective-permute-start | bytes 196616 | tf_op jit(solution)/shard_map/while/body/eval_jaxpr/ppermute | solution.py:10
  363.0 7.7 %collective-permute-start = (f32[16,1024]{1,0:T(8,128)S(1)}, f32[16,1024]{1,0:T(8,128)S(1)}, u32[]{:S(2)}, u32[]{:S(2)}) collective-permute-start(f32[16,1024]{1,0:T(8,128)S(1)} %multiply_add_fusion.2), channel_id=1, source_target_pairs={{0,8},{8,16},{16,24},{24,32},{32,40},{40,48},{48,56},{56,64},{64,7... | collective-permute-start | bytes 196616 | tf_op jit(solution)/shard_map/while/body/eval_jaxpr/ppermute | solution.py:10
  378.4 7.7 %collective-permute-start = (f32[16,1024]{1,0:T(8,128)S(1)}, f32[16,1024]{1,0:T(8,128)S(1)}, u32[]{:S(2)}, u32[]{:S(2)}) collective-permute-start(f32[16,1024]{1,0:T(8,128)S(1)} %multiply_add_fusion.2), channel_id=1, source_target_pairs={{0,8},{8,16},{16,24},{24,32},{32,40},{40,48},{48,56},{56,64},{64,7... | collective-permute-start | bytes 196616 | tf_op jit(solution)/shard_map/while/body/eval_jaxpr/ppermute | solution.py:10
  386.2 7.7 %collective-permute-start = (f32[16,1024]{1,0:T(8,128)S(1)}, f32[16,1024]{1,0:T(8,128)S(1)}, u32[]{:S(2)}, u32[]{:S(2)}) collective-permute-start(f32[16,1024]{1,0:T(8,128)S(1)} %multiply_add_fusion.2), channel_id=1, source_target_pairs={{0,8},{8,16},{16,24},{24,32},{32,40},{40,48},{48,56},{56,64},{64,7... | collective-permute-start | bytes 196616 | tf_op jit(solution)/shard_map/while/body/eval_jaxpr/ppermute | solution.py:10
  393.9 7.7 %collective-permute-start = (f32[16,1024]{1,0:T(8,128)S(1)}, f32[16,1024]{1,0:T(8,128)S(1)}, u32[]{:S(2)}, u32[]{:S(2)}) collective-permute-start(f32[16,1024]{1,0:T(8,128)S(1)} %multiply_add_fusion.2), channel_id=1, source_target_pairs={{0,8},{8,16},{16,24},{24,32},{32,40},{40,48},{48,56},{56,64},{64,7... | collective-permute-start | bytes 196616 | tf_op jit(solution)/shard_map/while/body/eval_jaxpr/ppermute | solution.py:10
  401.6 7.7 %collective-permute-start = (f32[16,1024]{1,0:T(8,128)S(1)}, f32[16,1024]{1,0:T(8,128)S(1)}, u32[]{:S(2)}, u32[]{:S(2)}) collective-permute-start(f32[16,1024]{1,0:T(8,128)S(1)} %multiply_add_fusion.2), channel_id=1, source_target_pairs={{0,8},{8,16},{16,24},{24,32},{32,40},{40,48},{48,56},{56,64},{64,7... | collective-permute-start | bytes 196616 | tf_op jit(solution)/shard_map/while/body/eval_jaxpr/ppermute | solution.py:10
  409.3 7.7 %collective-permute-start = (f32[16,1024]{1,0:T(8,128)S(1)}, f32[16,1024]{1,0:T(8,128)S(1)}, u32[]{:S(2)}, u32[]{:S(2)}) collective-permute-start(f32[16,1024]{1,0:T(8,128)S(1)} %multiply_add_fusion.2), channel_id=1, source_target_pairs={{0,8},{8,16},{16,24},{24,32},{32,40},{40,48},{48,56},{56,64},{64,7... | collective-permute-start | bytes 196616 | tf_op jit(solution)/shard_map/while/body/eval_jaxpr/ppermute | solution.py:10
  417.0 7.7 %collective-permute-start = (f32[16,1024]{1,0:T(8,128)S(1)}, f32[16,1024]{1,0:T(8,128)S(1)}, u32[]{:S(2)}, u32[]{:S(2)}) collective-permute-start(f32[16,1024]{1,0:T(8,128)S(1)} %multiply_add_fusion.2), channel_id=1, source_target_pairs={{0,8},{8,16},{16,24},{24,32},{32,40},{40,48},{48,56},{56,64},{64,7... | collective-permute-start | bytes 196616 | tf_op jit(solution)/shard_map/while/body/eval_jaxpr/ppermute | solution.py:10
  424.7 7.7 %collective-permute-start = (f32[16,1024]{1,0:T(8,128)S(1)}, f32[16,1024]{1,0:T(8,128)S(1)}, u32[]{:S(2)}, u32[]{:S(2)}) collective-permute-start(f32[16,1024]{1,0:T(8,128)S(1)} %multiply_add_fusion.2), channel_id=1, source_target_pairs={{0,8},{8,16},{16,24},{24,32},{32,40},{40,48},{48,56},{56,64},{64,7... | collective-permute-start | bytes 196616 | tf_op jit(solution)/shard_map/while/body/eval_jaxpr/ppermute | solution.py:10
  440.1 7.7 %collective-permute-start = (f32[16,1024]{1,0:T(8,128)S(1)}, f32[16,1024]{1,0:T(8,128)S(1)}, u32[]{:S(2)}, u32[]{:S(2)}) collective-permute-start(f32[16,1024]{1,0:T(8,128)S(1)} %multiply_add_fusion.2), channel_id=1, source_target_pairs={{0,8},{8,16},{16,24},{24,32},{32,40},{40,48},{48,56},{56,64},{64,7... | collective-permute-start | bytes 196616 | tf_op jit(solution)/shard_map/while/body/eval_jaxpr/ppermute | solution.py:10
  447.8 7.7 %collective-permute-start = (f32[16,1024]{1,0:T(8,128)S(1)}, f32[16,1024]{1,0:T(8,128)S(1)}, u32[]{:S(2)}, u32[]{:S(2)}) collective-permute-start(f32[16,1024]{1,0:T(8,128)S(1)} %multiply_add_fusion.2), channel_id=1, source_target_pairs={{0,8},{8,16},{16,24},{24,32},{32,40},{40,48},{48,56},{56,64},{64,7... | collective-permute-start | bytes 196616 | tf_op jit(solution)/shard_map/while/body/eval_jaxpr/ppermute | solution.py:10
  455.6 7.7 %collective-permute-start = (f32[16,1024]{1,0:T(8,128)S(1)}, f32[16,1024]{1,0:T(8,128)S(1)}, u32[]{:S(2)}, u32[]{:S(2)}) collective-permute-start(f32[16,1024]{1,0:T(8,128)S(1)} %multiply_add_fusion.2), channel_id=1, source_target_pairs={{0,8},{8,16},{16,24},{24,32},{32,40},{40,48},{48,56},{56,64},{64,7... | collective-permute-start | bytes 196616 | tf_op jit(solution)/shard_map/while/body/eval_jaxpr/ppermute | solution.py:10
  463.3 7.7 %collective-permute-start = (f32[16,1024]{1,0:T(8,128)S(1)}, f32[16,1024]{1,0:T(8,128)S(1)}, u32[]{:S(2)}, u32[]{:S(2)}) collective-permute-start(f32[16,1024]{1,0:T(8,128)S(1)} %multiply_add_fusion.2), channel_id=1, source_target_pairs={{0,8},{8,16},{16,24},{24,32},{32,40},{40,48},{48,56},{56,64},{64,7... | collective-permute-start | bytes 196616 | tf_op jit(solution)/shard_map/while/body/eval_jaxpr/ppermute | solution.py:10
  471.0 7.7 %collective-permute-start = (f32[16,1024]{1,0:T(8,128)S(1)}, f32[16,1024]{1,0:T(8,128)S(1)}, u32[]{:S(2)}, u32[]{:S(2)}) collective-permute-start(f32[16,1024]{1,0:T(8,128)S(1)} %multiply_add_fusion.2), channel_id=1, source_target_pairs={{0,8},{8,16},{16,24},{24,32},{32,40},{40,48},{48,56},{56,64},{64,7... | collective-permute-start | bytes 196616 | tf_op jit(solution)/shard_map/while/body/eval_jaxpr/ppermute | solution.py:10
  478.7 7.7 %collective-permute-start = (f32[16,1024]{1,0:T(8,128)S(1)}, f32[16,1024]{1,0:T(8,128)S(1)}, u32[]{:S(2)}, u32[]{:S(2)}) collective-permute-start(f32[16,1024]{1,0:T(8,128)S(1)} %multiply_add_fusion.2), channel_id=1, source_target_pairs={{0,8},{8,16},{16,24},{24,32},{32,40},{40,48},{48,56},{56,64},{64,7... | collective-permute-start | bytes 196616 | tf_op jit(solution)/shard_map/while/body/eval_jaxpr/ppermute | solution.py:10
  486.4 7.7 %collective-permute-start = (f32[16,1024]{1,0:T(8,128)S(1)}, f32[16,1024]{1,0:T(8,128)S(1)}, u32[]{:S(2)}, u32[]{:S(2)}) collective-permute-start(f32[16,1024]{1,0:T(8,128)S(1)} %multiply_add_fusion.2), channel_id=1, source_target_pairs={{0,8},{8,16},{16,24},{24,32},{32,40},{40,48},{48,56},{56,64},{64,7... | collective-permute-start | bytes 196616 | tf_op jit(solution)/shard_map/while/body/eval_jaxpr/ppermute | solution.py:10
  501.8 7.7 %collective-permute-start = (f32[16,1024]{1,0:T(8,128)S(1)}, f32[16,1024]{1,0:T(8,128)S(1)}, u32[]{:S(2)}, u32[]{:S(2)}) collective-permute-start(f32[16,1024]{1,0:T(8,128)S(1)} %multiply_add_fusion.2), channel_id=1, source_target_pairs={{0,8},{8,16},{16,24},{24,32},{32,40},{40,48},{48,56},{56,64},{64,7... | collective-permute-start | bytes 196616 | tf_op jit(solution)/shard_map/while/body/eval_jaxpr/ppermute | solution.py:10
  509.5 7.7 %collective-permute-start = (f32[16,1024]{1,0:T(8,128)S(1)}, f32[16,1024]{1,0:T(8,128)S(1)}, u32[]{:S(2)}, u32[]{:S(2)}) collective-permute-start(f32[16,1024]{1,0:T(8,128)S(1)} %multiply_add_fusion.2), channel_id=1, source_target_pairs={{0,8},{8,16},{16,24},{24,32},{32,40},{40,48},{48,56},{56,64},{64,7... | collective-permute-start | bytes 196616 | tf_op jit(solution)/shard_map/while/body/eval_jaxpr/ppermute | solution.py:10
  (24 other events, 1497.9 us)
Sparse Core Ops, SparseCore 0:
  526.0 180.7 all-reduce.1
where the time goes:
time: 721 us; the launch traced here: 717 us
  starting transfers between devices  381 us (53%)
  waiting for transfers between devices  263 us (36%)
  matrix products  28.9 us (4%)
  other arithmetic  17.8 us (2%)
  between operations  14.9 us (2%)
  local copies, waits for them, and re-layouts  10.4 us (1%)
    ppermute x64, starting transfers between devices, shifted(): return lax.ppermute(block, axis, route)  381 us
    psum x1, waiting for transfers between devices, local(): lax.psum(partial_logits.astype(jnp.bfloat16), 'chan').astype(jnp.float32)  181 us
    ppermute x64, waiting for transfers between devices, shifted(): return lax.ppermute(block, axis, route)  81.8 us
    dot_general x4, matrix products, block_states(): jnp.einsum('ts,psc->ptc', same_doc, weighted, precision=lax.Precision.HIG...  27.8 us
  transfers between devices with their start and end apart: 65, of which 64 were waited for; matrix products, arithmetic and copies ran while one was open for 1% of the time, Pallas kernels for 0%

commit v1 on v0

v1 whole, which is shorter than its diff:
```python
import functools

import jax
import jax.numpy as jnp
from jax import lax
from jax.experimental import pallas as pl
from jax.experimental.pallas import tpu as pltpu
from jax.sharding import PartitionSpec as P

F32 = jnp.float32
BF16 = jnp.bfloat16
LANES = 128
SUBS = 8
VMEM_LIMIT = 48 * 1024 * 1024


def start_positions(docs_ref, count):
    starts = [jnp.int32(0)]
    for i in range(count - 1):
        starts.append(starts[-1] + docs_ref[i])
    return starts


def no_start_in(starts, low, high):
    clean = jnp.float32(1.0)
    for s in starts:
        clean = jnp.where((s >= low) & (s < high), jnp.float32(0.0), clean)
    return clean


def keep_rows(starts, position):
    keep = jnp.ones(position.shape, F32)
    for s in starts:
        keep = jnp.where(position == s, 0.0, keep)
    return keep


def shifted_down(rows, top):
    sub = lax.broadcasted_iota(jnp.int32, rows.shape, 0)
    return jnp.where(sub == 0, top, pltpu.roll(rows, 1, 0))


def filter_steps(load, halo, taps, keep_at, keep_before, steps):
    last = load(steps - 1)
    previous = shifted_down(last, halo[1:2])
    masked_before = keep_before * shifted_down(load(steps - 2), halo[0:1])
    for j in range(steps):
        now = load(j)
        keep = keep_at(j)
        masked = keep * previous
        yield taps[0] * now + taps[1] * masked + taps[2] * (keep * masked_before)
        masked_before = masked
        previous = now


def first_kernel(
    docs_ref, first_ref, streams_ref, halo_ref, taps_ref, rates_ref,
    ends_ref, chunk_ref, driver_ref, query_ref,
    keep_scr, tail_scr, wide_scr, end_scr,
):
    poles, chans = rates_ref.shape
    block_len = streams_ref.shape[1]
    steps = block_len // SUBS
    first = first_ref[0]
    starts = start_positions(docs_ref, docs_ref.shape[0])
    base = first + steps * lax.broadcasted_iota(jnp.int32, (SUBS, LANES), 0)
    keep_before = keep_rows(starts, base - 1)
    tail = jnp.ones((SUBS, LANES), F32)
    for j in reversed(range(steps)):
        keep = keep_rows(starts, base + j)
        keep_scr[j * SUBS : (j + 1) * SUBS] = keep
        tail_scr[j * SUBS : (j + 1) * SUBS] = tail
        tail = tail * keep
    sub = lax.broadcasted_iota(jnp.int32, (SUBS, LANES), 0)
    reach = [tail]
    for k in (1, 2):
        reach.append(reach[-1] * jnp.where(sub >= k, pltpu.roll(reach[-1], k, 0), 0.0))
    reach = [jnp.where(sub >= k, r, 0.0) for k, r in zip((1, 2, 4), reach)]

    def group(g, carry):
        lanes = pl.ds(pl.multiple_of(g * LANES, LANES), LANES)
        for i in range(3):
            wide_scr[i] = streams_ref[i, :, lanes].astype(F32)

        def steps_of(i):
            halo = halo_ref[i, :, lanes].astype(F32)
            taps = [
                jnp.broadcast_to(taps_ref[i, n : n + 1, lanes], (SUBS, LANES)) for n in range(3)
            ]
            return filter_steps(
                lambda j: wide_scr[i, pl.ds(j, SUBS, stride=steps), :],
                halo,
                taps,
                lambda j: keep_scr[j * SUBS : (j + 1) * SUBS],
                keep_before,
                steps,
            )

        rate = [rates_ref[p : p + 1, lanes] for p in range(poles)]
        decay = [jnp.broadcast_to(jnp.exp(-r), (SUBS, LANES)) for r in rate]
        state = [jnp.zeros((SUBS, LANES), F32) for _ in range(poles)]
        for j, (key, value) in enumerate(zip(steps_of(1), steps_of(2))):
            rows = slice(j * SUBS, (j + 1) * SUBS)
            driver = key * value
            driver_ref[rows, lanes] = driver
            masked = driver * tail_scr[rows]
            state = [d * s + masked for d, s in zip(decay, state)]
        for j, query in enumerate(steps_of(0)):
            query_ref[j * SUBS : (j + 1) * SUBS, lanes] = query
        for p in range(poles):
            power = jnp.broadcast_to(jnp.exp(-steps * rate[p]), (SUBS, LANES))
            total = state[p]
            for k, r in zip((1, 2, 4), reach):
                total = total + (power * r) * pltpu.roll(total, k, 0)
                power = power * power
            chunk_ref[p, :, lanes] = total
            end_scr[p : p + 1, lanes] = total[SUBS - 1 : SUBS]
        return carry

    lax.fori_loop(0, chans // LANES, group, 0)
    ends = end_scr[...].astype(BF16)
    for i in range(ends_ref.shape[0]):
        ends_ref[i] = ends


def row_kernel(docs_ref, first_ref, rates_ref, ends_ref, totals_ref, before_ref, *, block_len):
    members = ends_ref.shape[0]
    first = first_ref[0]
    me = lax.rem(lax.div(first, block_len), members)
    row_first = first - me * block_len
    starts = start_positions(docs_ref, docs_ref.shape[0])
    transfer = jnp.exp(-rates_ref[...] * block_len)
    total = jnp.zeros(transfer.shape, F32)
    before = jnp.zeros(transfer.shape, F32)
    for j in range(members):
        before = jnp.where(me == j, total, before)
        low = row_first + j * block_len
        total = (transfer * no_start_in(starts, low, low + block_len)) * total + ends_ref[j].astype(F32)
    before_ref[...] = before
    rounded = total.astype(BF16)
    for i in range(totals_ref.shape[0]):
        totals_ref[i] = rounded


def out_kernel(
    docs_ref, first_ref, rates_ref, residues_ref, direct_ref, totals_ref, before_ref,
    chunk_ref, driver_ref, query_ref, unembed_ref,
    gated_ref, logits_ref,
    keep_scr, clean_scr, arriving_scr, out_scr,
    *, block_len, row_members,
):
    poles, chans = rates_ref.shape
    steps = block_len // SUBS
    first = first_ref[0]
    block = lax.div(first, block_len)
    row = lax.div(block, row_members)
    me = lax.rem(block, row_members)
    row_len = block_len * row_members
    starts = start_positions(docs_ref, docs_ref.shape[0])

    rates = rates_ref[...]
    row_transfer = jnp.exp(-rates * row_len)
    total = jnp.zeros(rates.shape, F32)
    for j in range(totals_ref.shape[0]):
        low = j * row_len
        clean = no_start_in(starts, low, low + row_len)
        moved = (row_transfer * clean) * total + totals_ref[j].astype(F32)
        total = jnp.where(j < row, moved, total)
    within = jnp.exp(-rates * (me * block_len).astype(F32)) * no_start_in(starts, row * row_len, first)
    arriving_scr[...] = before_ref[...] + within * total

    sub = lax.broadcasted_iota(jnp.int32, (SUBS, LANES), 0)
    base = first + steps * sub
    clean = jnp.ones((SUBS, LANES), F32)
    for j in range(steps):
        keep = keep_rows(starts, base + j)
        keep_scr[j * SUBS : (j + 1) * SUBS] = keep
    for s in starts:
        clean = jnp.where((s >= first) & (s < base), 0.0, clean)
    clean_scr[...] = clean

    def group(g, carry):
        lanes = pl.ds(pl.multiple_of(g * LANES, LANES), LANES)
        decay, weight, state = [], [], []
        for p in range(poles):
            rate = jnp.broadcast_to(rates_ref[p : p + 1, lanes], (SUBS, LANES))
            once = jnp.exp(-rate)
            decay.append(once)
            weight.append(residues_ref[p : p + 1, lanes] * (1.0 - once))
            carried = jnp.exp(-rate * (steps * sub).astype(F32)) * clean_scr[...]
            before = jnp.where(sub == 0, 0.0, pltpu.roll(chunk_ref[p, :, lanes], 1, 0))
            state.append(before + carried * arriving_scr[p : p + 1, lanes])
        direct = jnp.broadcast_to(direct_ref[0:1, lanes], (SUBS, LANES))
        for j in range(steps):
            rows = slice(j * SUBS, (j + 1) * SUBS)
            driver = driver_ref[rows, lanes]
            keep = keep_scr[rows]
            state = [d * (keep * s) + driver for d, s in zip(decay, state)]
            terms = [w * s for w, s in zip(weight, state)] + [direct * driver]
            while len(terms) > 1:
                paired = [a + b for a, b in zip(terms[::2], terms[1::2])]
                terms = paired + ([terms[-1]] if len(terms) % 2 else [])
            out_scr[pl.ds(j, SUBS, stride=steps), :] = query_ref[rows, lanes] * terms[0]
        gated_ref[:, lanes] = out_scr[...].astype(BF16)
        return carry

    lax.fori_loop(0, chans // LANES, group, 0)
    logits = jnp.dot(gated_ref[...], unembed_ref[...], preferred_element_type=F32).astype(BF16)
    share = logits_ref.shape[1]
    for i in range(logits_ref.shape[0]):
        logits_ref[i] = logits[i * share : (i + 1) * share]


def loss_kernel(place_ref, targets_ref, parts_ref, loss_ref):
    members, share, vocab = parts_ref.shape
    logits = parts_ref[0].astype(F32)
    for i in range(1, members):
        logits = logits + parts_ref[i].astype(F32)
    first = place_ref[0] * share
    row = lax.broadcasted_iota(jnp.int32, (share, 1), 0)
    target = jnp.zeros((share, 1), jnp.int32)
    for t in range(share):
        target = jnp.where(row == t, targets_ref[first + t], target)
    peak = jnp.max(logits, axis=1, keepdims=True)
    total = jnp.sum(jnp.exp(logits - peak), axis=1, keepdims=True)
    ids = lax.broadcasted_iota(jnp.int32, logits.shape, 1)
    picked = jnp.sum(jnp.where(ids == target, logits, 0.0), axis=1, keepdims=True)
    loss = peak + jnp.log(total) - picked
    spread = lax.broadcasted_iota(jnp.int32, (share, share), 0) == lax.broadcasted_iota(
        jnp.int32, (share, share), 1
    )
    line = jnp.sum(jnp.where(spread, loss, 0.0), axis=0, keepdims=True)
    for i in range(loss_ref.shape[0]):
        loss_ref[i] = line


def in_vmem(count):
    return [pl.BlockSpec(memory_space=pltpu.VMEM)] * count


def in_smem(count):
    return [pl.BlockSpec(memory_space=pltpu.SMEM)] * count


PARAMS = pltpu.CompilerParams(vmem_limit_bytes=VMEM_LIMIT)


def local(row_members, streams, short_filter, pole_rates, residues, direct, doc_lengths, targets, unembed):
    block_len, chans = streams.shape[1:]
    poles = pole_rates.shape[0]
    vocab = unembed.shape[1]
    seq, chan = lax.axis_size("seq"), lax.axis_size("chan")
    rows = seq // row_members
    share = block_len // chan
    steps = block_len // SUBS
    block = lax.axis_index("seq")
    first = (block * block_len).astype(jnp.int32).reshape(1)
    place = lax.axis_index("chan").astype(jnp.int32).reshape(1)
    halo = lax.ppermute(
        streams[:, block_len - 2 :, :], "seq", [(i, i + 1) for i in range(seq - 1)]
    )
    ends, chunks, driver, query = pl.pallas_call(
        first_kernel,
        out_shape=(
            jax.ShapeDtypeStruct((row_members, poles, chans), BF16),
            jax.ShapeDtypeStruct((poles, SUBS, chans), F32),
            jax.ShapeDtypeStruct((block_len, chans), F32),
            jax.ShapeDtypeStruct((block_len, chans), F32),
        ),
        in_specs=in_smem(2) + in_vmem(4),
        out_specs=in_vmem(4),
        scratch_shapes=[
            pltpu.VMEM((block_len, LANES), F32),
            pltpu.VMEM((block_len, LANES), F32),
            pltpu.VMEM((3, block_len, LANES), F32),
            pltpu.VMEM((poles, chans), F32),
        ],
        compiler_params=PARAMS,
        name="block_states",
    )(doc_lengths, first, streams, halo, short_filter, pole_rates)
    along_row = [[r * row_members + i for i in range(row_members)] for r in range(rows)]
    across_rows = [[r * row_members + i for r in range(rows)] for i in range(row_members)]
    ends = lax.all_to_all(ends, "seq", 0, 0, axis_index_groups=along_row)
    totals, before = pl.pallas_call(
        functools.partial(row_kernel, block_len=block_len),
        out_shape=(
            jax.ShapeDtypeStruct((rows, poles, chans), BF16),
            jax.ShapeDtypeStruct((poles, chans), F32),
        ),
        in_specs=in_smem(2) + in_vmem(2),
        out_specs=in_vmem(2),
        compiler_params=PARAMS,
        name="row_states",
    )(doc_lengths, first, pole_rates, ends)
    totals = lax.all_to_all(totals, "seq", 0, 0, axis_index_groups=across_rows)
    gated, logits = pl.pallas_call(
        functools.partial(out_kernel, block_len=block_len, row_members=row_members),
        out_shape=(
            jax.ShapeDtypeStruct((block_len, chans), BF16),
            jax.ShapeDtypeStruct((chan, share, vocab), BF16),
        ),
        in_specs=in_smem(2) + in_vmem(9),
        out_specs=in_vmem(2),
        scratch_shapes=[
            pltpu.VMEM((block_len, LANES), F32),
            pltpu.VMEM((SUBS, LANES), F32),
            pltpu.VMEM((poles, chans), F32),
            pltpu.VMEM((block_len, LANES), F32),
        ],
        compiler_params=PARAMS,
        name="gated_logits",
    )(
        doc_lengths, first, pole_rates, residues, direct[None], totals, before,
        chunks, driver, query, unembed,
    )
    parts = lax.all_to_all(logits, "chan", 0, 0)
    losses = pl.pallas_call(
        loss_kernel,
        out_shape=jax.ShapeDtypeStruct((chan, 1, share), F32),
        in_specs=in_smem(2) + in_vmem(1),
        out_specs=pl.BlockSpec(memory_space=pltpu.VMEM),
        compiler_params=PARAMS,
        name="token_losses",
    )(place, targets, parts)
    losses = lax.all_to_all(losses, "chan", 0, 0)
    return gated, losses.reshape(block_len)


def solution(mesh):
    seq = mesh.shape["seq"]
    row_members = 8 if seq % 8 == 0 else seq
    in_specs = (
        P(None, "seq", "chan"),
        P(None, None, "chan"),
        P(None, "chan"),
        P(None, "chan"),
        P("chan"),
        P(),
        P("seq"),
        P("chan", None),
    )
    out_specs = (P("seq", "chan"), P("seq"))
    return jax.shard_map(
        functools.partial(local, row_members),
        mesh=mesh,
        in_specs=in_specs,
        out_specs=out_specs,
        check_vma=False,
    )
```

time: 721 us -> 85.2 us (0.12)
  starting transfers between devices: 381 us -> 12.2 us
  waiting for transfers between devices: 263 us -> 13.6 us
  blocking collectives: 0 us -> 40.8 us
  matrix products: 28.9 us -> 0 us
  other arithmetic: 17.8 us -> 0.66 us
  between operations: 14.9 us -> 0.7 us
  Pallas kernels: 0 us -> 11 us
    ppermute x64 -> x1, starting transfers between devices: 381 us -> 1.92 us  [local(): lax.ppermute(streams[:, block_len - 2:, :], 'seq', [(i, i + 1) for i in r...]
    psum x1 -> x0, waiting for transfers between devices: 181 us -> none  [local(): lax.psum(partial_logits.astype(jnp.bfloat16), 'chan').astype(jnp.float32)]
    ppermute x64 -> x1, waiting for transfers between devices: 81.8 us -> 3.08 us  [local(): lax.ppermute(streams[:, block_len - 2:, :], 'seq', [(i, i + 1) for i in r...]
    all_to_all x0 -> x3, blocking collectives: none -> 40.8 us  [the longest x1 19.3 us: local(): totals = lax.all_to_all(totals, 'seq', 0, 0, axis_index_groups=across_rows)]
    dot_general x5 -> x0, matrix products: 28.9 us -> none  [the longest x4 27.8 us: block_states(): jnp.einsum('ts,psc->ptc', same_doc, weighted, precision=lax.Precision.HIG...]
    pallas_call x0 -> x4, Pallas kernels: none -> 11 us  [the longest x1 5.22 us: local(): pl.pallas_call(functools.partial(out_kernel, block_len=block_len, row_mem...]
    all_to_all x0 -> x1, waiting for transfers between devices: none -> 10.5 us  [local(): parts = lax.all_to_all(logits, 'chan', 0, 0)]
    all_to_all x0 -> x1, starting transfers between devices: none -> 10.3 us  [local(): parts = lax.all_to_all(logits, 'chan', 0, 0)]
  transfers between devices with their start and end apart: 65 -> 2, of which waited for: 64 -> 2; matrix products, arithmetic and copies ran while one was open for 1% -> 0% of each run, Pallas kernels for 0% -> 0%
where the time goes in v1:
time: 85.2 us; the launch traced here: 84.7 us
  blocking collectives  40.8 us (48%)
  waiting for transfers between devices  13.6 us (16%)
  starting transfers between devices  12.2 us (14%)
  Pallas kernels  11 us (13%)
  local copies, waits for them, and re-layouts  5.69 us (7%)
    all_to_all x1, blocking collectives, local(): totals = lax.all_to_all(totals, 'seq', 0, 0, axis_index_groups=across_rows)  19.3 us
    all_to_all x1, blocking collectives, local(): ends = lax.all_to_all(ends, 'seq', 0, 0, axis_index_groups=along_row)  11.5 us
    all_to_all x1, waiting for transfers between devices, local(): parts = lax.all_to_all(logits, 'chan', 0, 0)  10.5 us
    all_to_all x1, starting transfers between devices, local(): parts = lax.all_to_all(logits, 'chan', 0, 0)  10.3 us
    all_to_all x1, blocking collectives, local(): losses = lax.all_to_all(losses, 'chan', 0, 0)  10 us
    pallas_call x1, Pallas kernels, local(): pl.pallas_call(functools.partial(out_kernel, block_len=block_len, row_mem...  5.22 us
    pallas_call x1, Pallas kernels, local(): pl.pallas_call(first_kernel, out_shape=(jax.ShapeDtypeStruct((row_members...  4.39 us
    unnamed x16, local copies, waits for them, and re-layouts  3.72 us
  transfers between devices with their start and end apart: 2, of which 2 were waited for; matrix products, arithmetic and copies ran while one was open for 0% of the time, Pallas kernels for 0%

profile of v1, /device:TPU:2, one launch (start us, length us, event | category | flops | bytes accessed | tf_op | source)
XLA Modules:
  0.0 84.7 jit_solution(2806948245229311183)
XLA Ops:
  0.6 0.0 copy-start.6
  0.6 0.8 slice.3
  1.5 1.9 %collective-permute-start = (bf16[3,2,1024]{2,1,0:T(2,128)(2,1)S(1)}, bf16[3,2,1024]{2,1,0:T(2,128)(2,1)S(1)}, u32[]{:S(2)}, u32[]{:S(2)}) collective-permute-start(bf16[3,2,1024]{2,1,0:T(2,128)(2,1)S(1)} %slice.3), channel_id=1, source_target_pairs={{0,8},{8,16},{16,24},{24,32},{32,40},{40,48},{48,56},{56,64},{64,7... | collective-permute-start | bytes 36872 | tf_op jit(solution)/shard_map/ppermute | solution.py:259
  3.4 3.1 %collective-permute-done.halo_ref = bf16[3,2,1024]{2,1,0:T(2,128)(2,1)S(1)} collective-permute-done((bf16[3,2,1024]{2,1,0:T(2,128)(2,1)S(1)}, bf16[3,2,1024]{2,1,0:T(2,128)(2,1)S(1)}, u32[]{:S(2)}, u32[]{:S(2)}) %collective-permute-start) | collective-permute-done | bytes 12320 | tf_op jit(solution)/shard_map/ppermute | solution.py:259
  6.5 0.0 copy-start
  6.5 1.4 %copy-done = bf16[3,256,1024]{2,1,0:T(8,128)(2,1)S(1)} copy-done((bf16[3,256,1024]{2,1,0:T(8,128)(2,1)S(1)}, bf16[3,256,1024]{2,1,0:T(8,128)(2,1)}, u32[]{:S(2)}) %copy-start) | copy-done | bytes 1572888
  7.9 0.0 copy-start.2
  7.9 0.8 copy-done.2
  8.7 0.0 copy-start.4
  8.7 0.8 copy-done.4
  9.5 0.0 copy-start.5
  9.5 0.7 copy-done.5
  10.2 0.0 copy-start.1
  10.2 0.0 copy-start.3
  10.2 4.4 %block_states.1 = (bf16[8,16,1024]{2,1,0:T(8,128)(2,1)S(1)}, f32[16,8,1024]{2,1,0:T(8,128)S(1)}, f32[256,1024]{1,0:T(8,128)S(1)}, f32[256,1024]{1,0:T(8,128)S(1)}) custom-call(s32[4]{0:T(128)S(1)} %copy-done.5, s32[1]{0:T(128)} %bitcast.first_ref, bf16[3,256,1024]{2,1,0:T(8,128)(2,1)S(1)} %copy-done, bf16[3,2,1024]{2,1,0:T(2,128)(2,1)S(1)} %collective-permute-done.halo_ref, ...), custom_call_target="tpu_custom_call" | custom-call | tf_op jit(solution)/shard_map/block_states/pallas_call | solution.py:262
  14.6 11.5 %all_to_all.20.ends_ref = bf16[8,16,1024]{2,1,0:T(8,128)(2,1)S(1)} all-to-all(bf16[8,16,1024]{2,1,0:T(8,128)(2,1)S(1)} %get-tuple-element.10), channel_id=1, replica_groups={{0,8,16,24,32,40,48,56},{64,72,80,88,96,104,112,120},{128,136,144,152,1..., dimensions={0} | all-to-all | bytes 524288 | tf_op jit(solution)/shard_map/all_to_all | solution.py:283
  26.1 0.7 row_states.1
  26.7 19.3 %all_to_all.21.totals_ref = bf16[8,16,1024]{2,1,0:T(8,128)(2,1)S(1)} all-to-all(bf16[8,16,1024]{2,1,0:T(8,128)(2,1)S(1)} %get-tuple-element.11), channel_id=1, replica_groups={{0,64,128,192,256,320,384,448},{8,72,136,200,264,328,392,456},{16,80,14..., dimensions={0} | all-to-all | bytes 524288 | tf_op jit(solution)/shard_map/all_to_all | solution.py:295
  46.0 0.0 copy-done.6
  46.0 0.0 copy-done.1
  46.0 0.0 copy-done.3
  46.0 0.0 copy-start.7
  46.0 5.2 %gated_logits.1 = (bf16[256,1024]{1,0:T(8,128)(2,1)}, bf16[8,32,512]{2,1,0:T(8,128)(2,1)}) custom-call(s32[4]{0:T(128)S(1)} %copy-done.5, s32[1]{0:T(128)} %bitcast.first_ref, f32[16,1024]{1,0:T(8,128)S(1)} %copy-done.2, f32[16,1024]{1,0:T(8,128)S(1)} %copy-done.3, f32[1,1024]{1,0:T(1,128)S(1)} %bitcast.3, bf16[8,16,1024]{2,1,0:T(8,128)(2,1)S(1)} %all_to_all.21.totals_ref, ...), custom_call_target="tpu_custom_call" | custom-call | tf_op jit(solution)/shard_map/gated_logits/pallas_call | solution.py:296
  51.2 10.3 %all-to-all-start.2 = ((bf16[8,32,512]{2,1,0:T(8,128)(2,1)}), bf16[8,32,512]{2,1,0:T(8,128)(2,1)S(1)}, u32[]{:S(2)}, u32[]{:S(2)}) async-start(bf16[8,32,512]{2,1,0:T(8,128)(2,1)} %get-tuple-element.17), calls=%async_computation.2 | async-start | bytes 524288 | tf_op jit(solution)/shard_map/all_to_all | solution.py:316
  61.5 10.5 %all-to-all-done.2.parts_ref = bf16[8,32,512]{2,1,0:T(8,128)(2,1)S(1)} async-done(((bf16[8,32,512]{2,1,0:T(8,128)(2,1)}), bf16[8,32,512]{2,1,0:T(8,128)(2,1)S(1)}, u32[]{:S(2)}, u32[]{:S(2)}) %all-to-all-start.2) | async-done | bytes 262176 | tf_op jit(solution)/shard_map/all_to_all | solution.py:316
  72.0 0.0 copy-done.7
  72.0 0.8 token_losses.1
  72.8 10.0 %all_to_all.22 = f32[8,1,32]{2,1,0:T(1,128)S(1)} all-to-all(f32[8,1,32]{2,1,0:T(1,128)S(1)} %token_losses.1), channel_id=1, replica_groups=mesh['seq'=64,'chan'=8] {'chan'}, dimensions={0} | all-to-all | bytes 2048 | tf_op jit(solution)/shard_map/all_to_all | solution.py:325
  82.8 0.5 broadcast.3
  83.4 0.7 reduce.3
  84.0 0.6 reshape.15
Async XLA Ops:
  0.6 45.4 %copy-start.6 = (f32[1024]{0:T(1024)S(1)}, f32[1024]{0:T(1024)}, u32[]{:S(2)}) copy-start(f32[1024]{0:T(1024)} %param.12) | copy-start | bytes 12292
  1.5 5.0 %collective-permute-start = (bf16[3,2,1024]{2,1,0:T(2,128)(2,1)S(1)}, bf16[3,2,1024]{2,1,0:T(2,128)(2,1)S(1)}, u32[]{:S(2)}, u32[]{:S(2)}) collective-permute-start(bf16[3,2,1024]{2,1,0:T(2,128)(2,1)S(1)} %slice.3), channel_id=1, source_target_pairs={{0,8},{8,16},{16,24},{24,32},{32,40},{40,48},{48,56},{56,64},{64,7... | collective-permute-start | bytes 36872 | tf_op jit(solution)/shard_map/ppermute | solution.py:259
  6.5 1.4 %copy-start = (bf16[3,256,1024]{2,1,0:T(8,128)(2,1)S(1)}, bf16[3,256,1024]{2,1,0:T(8,128)(2,1)}, u32[]{:S(2)}) copy-start(bf16[3,256,1024]{2,1,0:T(8,128)(2,1)} %streams_ref.1) | copy-start | bytes 4718596
  7.9 0.8 copy-start.2
  8.7 0.8 copy-start.4
  9.5 0.7 copy-start.5
  10.2 35.8 %copy-start.1 = (bf16[1024,512]{1,0:T(8,128)(2,1)S(1)}, bf16[1024,512]{1,0:T(8,128)(2,1)}, u32[]{:S(2)}) copy-start(bf16[1024,512]{1,0:T(8,128)(2,1)} %unembed_ref.1) | copy-start | bytes 3145732
  10.2 35.8 %copy-start.3 = (f32[16,1024]{1,0:T(8,128)S(1)}, f32[16,1024]{1,0:T(8,128)}, u32[]{:S(2)}) copy-start(f32[16,1024]{1,0:T(8,128)} %residues_ref.1) | copy-start | bytes 196612
  46.0 26.0 %copy-start.7 = (s32[256]{0:T(256)S(1)}, s32[256]{0:T(256)}, u32[]{:S(2)}) copy-start(s32[256]{0:T(256)} %targets_ref.1) | copy-start | bytes 3076
  51.2 20.8 %all-to-all-start.2 = ((bf16[8,32,512]{2,1,0:T(8,128)(2,1)}), bf16[8,32,512]{2,1,0:T(8,128)(2,1)S(1)}, u32[]{:S(2)}, u32[]{:S(2)}) async-start(bf16[8,32,512]{2,1,0:T(8,128)(2,1)} %get-tuple-element.17), calls=%async_computation.2 | async-start | bytes 524288 | tf_op jit(solution)/shard_map/all_to_all | solution.py:316

commit v2 on v1

v2 whole, which is shorter than its diff:
```python
import functools

import jax
import jax.numpy as jnp
from jax import lax
from jax.experimental import pallas as pl
from jax.experimental.pallas import tpu as pltpu
from jax.sharding import PartitionSpec as P

F32 = jnp.float32
BF16 = jnp.bfloat16
LANES = 128
SUBS = 8
PITCH = 40
VMEM_LIMIT = 16 * 1024 * 1024


def start_positions(docs_ref, count):
    starts = [jnp.int32(0)]
    for i in range(count - 1):
        starts.append(starts[-1] + docs_ref[i])
    return starts


def no_start_in(starts, low, high):
    clean = jnp.float32(1.0)
    for s in starts:
        clean = jnp.where((s >= low) & (s < high), jnp.float32(0.0), clean)
    return clean


def keep_rows(starts, position):
    keep = jnp.ones(position.shape, F32)
    for s in starts:
        keep = jnp.where(position == s, 0.0, keep)
    return keep


def shifted_down(rows, top):
    sub = lax.broadcasted_iota(jnp.int32, rows.shape, 0)
    return jnp.where(sub == 0, top, pltpu.roll(rows, 1, 0))


def filter_steps(load, halo, taps, keep_at, keep_before, steps):
    last = load(steps - 1)
    previous = shifted_down(last, halo[1:2])
    masked_before = keep_before * shifted_down(load(steps - 2), halo[0:1])
    for j in range(steps):
        now = load(j)
        keep = keep_at(j)
        masked = keep * previous
        yield taps[0] * now + taps[1] * masked + taps[2] * (keep * masked_before)
        masked_before = masked
        previous = now


def first_kernel(
    docs_hbm, streams_hbm, taps_hbm, rates_hbm,
    work_ref,
    docs_ref, streams_ref, taps_ref, rates_ref, keep_scr, tail_scr, wide_scr, sems, group_sems,
):
    poles, chans = rates_ref.shape
    block_len = streams_ref.shape[1]
    steps = block_len // SUBS
    groups = chans // LANES
    copies = [
        pltpu.make_async_copy(docs_hbm, docs_ref, sems.at[0]),
        pltpu.make_async_copy(taps_hbm, taps_ref, sems.at[1]),
        pltpu.make_async_copy(rates_hbm, rates_ref, sems.at[2]),
    ]

    def group_copy(g):
        lanes = pl.ds(pl.multiple_of(g * LANES, LANES), LANES)
        return pltpu.make_async_copy(
            streams_hbm.at[1:3, :, lanes], streams_ref.at[:, :, lanes], group_sems.at[g]
        )

    for c in copies:
        c.start()
    for g in range(groups):
        group_copy(g).start()
    first = lax.axis_index("seq") * block_len
    for c in copies:
        c.wait()
    starts = start_positions(docs_ref, docs_ref.shape[0])
    base = first + steps * lax.broadcasted_iota(jnp.int32, (SUBS, LANES), 0)
    keep_before = keep_rows(starts, base - 1)
    tail = jnp.ones((SUBS, LANES), F32)
    for j in reversed(range(steps)):
        keep = keep_rows(starts, base + j)
        keep_scr[j * SUBS : (j + 1) * SUBS] = keep
        tail_scr[j * SUBS : (j + 1) * SUBS] = tail
        tail = tail * keep
    nothing = jnp.zeros((2, LANES), F32)

    def group(g, carry):
        group_copy(g).wait()
        lanes = pl.ds(pl.multiple_of(g * LANES, LANES), LANES)
        for i in range(2):
            for s in range(SUBS):
                wide_scr[i, s * PITCH : s * PITCH + steps] = streams_ref[
                    i, s * steps : (s + 1) * steps, lanes
                ].astype(F32)

        def steps_of(i):
            taps = [
                jnp.broadcast_to(taps_ref[i + 1, n : n + 1, lanes], (SUBS, LANES))
                for n in range(3)
            ]
            return filter_steps(
                lambda j: wide_scr[i, pl.ds(j, SUBS, stride=PITCH), :],
                nothing,
                taps,
                lambda j: keep_scr[j * SUBS : (j + 1) * SUBS],
                keep_before,
                steps,
            )

        decay = [
            jnp.broadcast_to(jnp.exp(-rates_ref[p : p + 1, lanes]), (SUBS, LANES))
            for p in range(poles)
        ]
        state = [jnp.zeros((SUBS, LANES), F32) for _ in range(poles)]
        for j, (key, value) in enumerate(zip(steps_of(0), steps_of(1))):
            rows = slice(j * SUBS, (j + 1) * SUBS)
            if j < 2:
                work_ref[block_len + j : block_len + 1 + j, lanes] = key[0:1]
                work_ref[block_len + 2 + j : block_len + 3 + j, lanes] = value[0:1]
            driver = key * value
            work_ref[rows, lanes] = driver
            masked = driver * tail_scr[rows]
            state = [d * s + masked for d, s in zip(decay, state)]
        for p in range(poles):
            at = block_len + SUBS * (1 + p)
            work_ref[at : at + SUBS, lanes] = state[p]
        return carry

    lax.fori_loop(0, groups, group, 0)


def corrected(starts, first, steps, halo_ref, taps_ref, edge):
    older = no_start_in(starts, first - 1, first)
    keep = [no_start_in(starts, first + j, first + j + 1) for j in range(2)]

    def added(i):
        halo = halo_ref[i].astype(F32)
        taps = taps_ref[i]
        near = (keep[0] * taps[1:2]) * halo[1:2] + (keep[0] * older * taps[2:3]) * halo[0:1]
        return near, (keep[1] * keep[0] * taps[2:3]) * halo[1:2]

    key, value = added(1), added(2)
    drivers, changes = [], []
    for j in range(2):
        old_key, old_value = edge[j : j + 1], edge[2 + j : 3 + j]
        driver = (old_key + key[j]) * (old_value + value[j])
        counts = no_start_in(starts, first + j + 1, first + steps)
        drivers.append(driver)
        changes.append(counts * (driver - old_key * old_value))
    return drivers, changes


def chunk_reach(starts, first, steps):
    sub = lax.broadcasted_iota(jnp.int32, (SUBS, LANES), 0)
    base = first + steps * sub
    clean = jnp.ones((SUBS, LANES), F32)
    for s in starts:
        clean = jnp.where((s >= base) & (s < base + steps), 0.0, clean)
    reach = [clean]
    for k in (1, 2):
        reach.append(reach[-1] * jnp.where(sub >= k, pltpu.roll(reach[-1], k, 0), 0.0))
    return [jnp.where(sub >= k, r, 0.0) for k, r in zip((1, 2, 4), reach)]


def chunk_ends(state, young, power, reach):
    sub = lax.broadcasted_iota(jnp.int32, (SUBS, LANES), 0)
    total = state + jnp.where(sub == 0, young, 0.0)
    power = jnp.broadcast_to(power, (SUBS, LANES))
    for k, r in zip((1, 2, 4), reach):
        total = total + (power * r) * pltpu.roll(total, k, 0)
        power = power * power
    return total


def join_kernel(
    docs_ref, halo_ref, taps_ref, rates_ref, residues_ref, work_ref,
    ends_ref, old_scr, young_scr, end_scr,
    *, block_len,
):
    poles, chans = rates_ref.shape
    steps = block_len // SUBS
    first = lax.axis_index("seq") * block_len
    starts = start_positions(docs_ref, docs_ref.shape[0])
    edge = work_ref[block_len : block_len + SUBS]
    _, changes = corrected(starts, first, steps, halo_ref, taps_ref, edge)
    rates = rates_ref[...]
    young_scr[...] = jnp.exp(-rates * (steps - 1)) * changes[0] + jnp.exp(-rates * (steps - 2)) * changes[1]
    old_scr[...] = jnp.exp(-rates * steps)
    reach = chunk_reach(starts, first, steps)
    for g in range(chans // LANES):
        lanes = slice(g * LANES, (g + 1) * LANES)
        for p in range(poles):
            at = block_len + SUBS * (1 + p)
            total = chunk_ends(
                work_ref[at : at + SUBS, lanes],
                young_scr[p : p + 1, lanes],
                old_scr[p : p + 1, lanes],
                reach,
            )
            end_scr[p : p + 1, lanes] = total[SUBS - 1 : SUBS]
    decays = jnp.exp(-rates)
    ends = (residues_ref[...] * ((1.0 - decays) * decays) * end_scr[...]).astype(BF16)
    for i in range(ends_ref.shape[0]):
        ends_ref[i] = ends


def row_kernel(docs_ref, rates_ref, ends_ref, totals_ref, *, block_len):
    members = ends_ref.shape[0]
    block = lax.axis_index("seq")
    first = block * block_len
    me = lax.rem(block, members)
    row_first = first - me * block_len
    starts = start_positions(docs_ref, docs_ref.shape[0])
    transfer = jnp.exp(-rates_ref[...] * block_len)
    total = jnp.zeros(transfer.shape, F32)
    before = jnp.zeros(transfer.shape, F32)
    for j in range(members):
        before = jnp.where(me == j, total, before)
        low = row_first + j * block_len
        total = (transfer * no_start_in(starts, low, low + block_len)) * total + ends_ref[j].astype(F32)
    row = lax.div(block, members)
    for i in range(totals_ref.shape[0]):
        totals_ref[i] = jnp.where(row == i, before, total).astype(BF16)


def local_kernel(
    docs_ref, halo_ref, work_ref, streams_hbm, taps_hbm, rates_hbm, residues_hbm, direct_hbm,
    made_ref,
    stream_ref, taps_ref, rates_ref, residues_ref, direct_ref,
    keep_scr, alive_scr, weight_scr, old_scr, young_scr, first_scr, wide_scr, local_scr, sems,
    *, block_len,
):
    poles, chans = rates_ref.shape
    steps = block_len // SUBS
    copies = [
        pltpu.make_async_copy(source, target, sems.at[i])
        for i, (source, target) in enumerate(
            (
                (taps_hbm, taps_ref),
                (rates_hbm, rates_ref),
                (residues_hbm, residues_ref),
                (direct_hbm, direct_ref),
                (streams_hbm.at[0], stream_ref),
            )
        )
    ]
    for c in copies:
        c.start()
    first = lax.axis_index("seq") * block_len
    starts = start_positions(docs_ref, docs_ref.shape[0])
    sub = lax.broadcasted_iota(jnp.int32, (SUBS, LANES), 0)
    base = first + steps * sub
    for j in range(steps):
        rows = slice(j * SUBS, (j + 1) * SUBS)
        keep_scr[rows] = keep_rows(starts, base + j)
        alive = jnp.ones((SUBS, LANES), F32)
        for s in starts:
            alive = jnp.where((s >= first) & (base + j >= s), 0.0, alive)
        alive_scr[rows] = alive
    keep_before = keep_rows(starts, base - 1)
    reach = chunk_reach(starts, first, steps)
    for c in copies:
        c.wait()
    edge = work_ref[block_len : block_len + SUBS]
    drivers, changes = corrected(starts, first, steps, halo_ref, taps_ref, edge)
    rates = rates_ref[...]
    decays = jnp.exp(-rates)
    weight_scr[...] = residues_ref[...] * (1.0 - decays)
    young_scr[...] = jnp.exp(-rates * (steps - 1)) * changes[0] + jnp.exp(-rates * (steps - 2)) * changes[1]
    old_scr[...] = jnp.exp(-rates * steps)
    for j in range(2):
        first_scr[j : j + 1] = drivers[j]

    def group(g, carry):
        lanes = pl.ds(pl.multiple_of(g * LANES, LANES), LANES)
        for s in range(SUBS):
            wide_scr[s * PITCH : s * PITCH + steps] = stream_ref[
                s * steps : (s + 1) * steps, lanes
            ].astype(F32)
        decay, weight, state = [], [], []
        for p in range(poles):
            rate = jnp.broadcast_to(rates_ref[p : p + 1, lanes], (SUBS, LANES))
            decay.append(jnp.exp(-rate))
            weight.append(jnp.broadcast_to(weight_scr[p : p + 1, lanes], (SUBS, LANES)))
            at = block_len + SUBS * (1 + p)
            total = chunk_ends(
                work_ref[at : at + SUBS, lanes],
                young_scr[p : p + 1, lanes],
                old_scr[p : p + 1, lanes],
                reach,
            )
            state.append(jnp.where(sub == 0, 0.0, pltpu.roll(total, 1, 0)))
        direct = jnp.broadcast_to(direct_ref[0:1, lanes], (SUBS, LANES))
        for j in range(steps):
            rows = slice(j * SUBS, (j + 1) * SUBS)
            driver = work_ref[rows, lanes]
            if j < 2:
                driver = jnp.where(sub == 0, first_scr[j : j + 1, lanes], driver)
            keep = keep_scr[rows]
            state = [d * (keep * s) + driver for d, s in zip(decay, state)]
            local_scr[rows] = summed(
                [w * s for w, s in zip(weight, state)] + [direct * driver]
            )
        taps = [jnp.broadcast_to(taps_ref[0, n : n + 1, lanes], (SUBS, LANES)) for n in range(3)]
        queries = filter_steps(
            lambda j: wide_scr[pl.ds(j, SUBS, stride=PITCH), :],
            halo_ref[0, :, lanes].astype(F32),
            taps,
            lambda j: keep_scr[j * SUBS : (j + 1) * SUBS],
            keep_before,
            steps,
        )
        local, asked = [], []
        for j, query in enumerate(queries):
            rows = slice(j * SUBS, (j + 1) * SUBS)
            local.append(query * local_scr[rows])
            asked.append(query * alive_scr[rows])
            if j % 2 == 1:
                rows = slice((j - 1) * SUBS, (j + 1) * SUBS)
                made_ref[0, rows, lanes] = jnp.concatenate(local).astype(BF16)
                made_ref[1, rows, lanes] = jnp.concatenate(asked).astype(BF16)
                local, asked = [], []
        return carry

    lax.fori_loop(0, chans // LANES, group, 0)


def summed(terms):
    while len(terms) > 1:
        paired = [a + b for a, b in zip(terms[::2], terms[1::2])]
        terms = paired + ([terms[-1]] if len(terms) % 2 else [])
    return terms[0]


def out_kernel(
    docs_ref, totals_ref, rates_ref, made_ref, unembed_hbm,
    gated_hbm, logits_ref,
    unembed_ref, gated_ref, arriving_scr, out_scr, sum_scr, sem, gated_sems,
    *, block_len, row_members,
):
    poles, chans = rates_ref.shape
    steps = block_len // SUBS
    groups = chans // LANES
    copy = pltpu.make_async_copy(unembed_hbm, unembed_ref, sem)
    gated_copies = []
    copy.start()
    block = lax.axis_index("seq")
    first = block * block_len
    row = lax.div(block, row_members)
    me = lax.rem(block, row_members)
    row_len = block_len * row_members
    starts = start_positions(docs_ref, docs_ref.shape[0])

    rates = rates_ref[...]
    row_transfer = jnp.exp(-rates * row_len)
    total = jnp.zeros(rates.shape, F32)
    before = jnp.zeros(rates.shape, F32)
    for j in range(totals_ref.shape[0]):
        low = j * row_len
        clean = no_start_in(starts, low, low + row_len)
        arrived = totals_ref[j].astype(F32)
        before = jnp.where(j == row, arrived, before)
        total = jnp.where(j < row, (row_transfer * clean) * total + arrived, total)
    within = jnp.exp(-rates * (me * block_len).astype(F32)) * no_start_in(
        starts, row * row_len, first
    )
    arriving_scr[...] = before + within * total
    sub = lax.broadcasted_iota(jnp.int32, (SUBS, LANES), 0)

    share = logits_ref.shape[1]
    for g in range(groups):
        lanes = slice(g * LANES, (g + 1) * LANES)
        decay, fading = [], []
        for p in range(poles):
            rate = jnp.broadcast_to(rates_ref[p : p + 1, lanes], (SUBS, LANES))
            decay.append(jnp.exp(-rate))
            fading.append(
                jnp.exp(-rate * (steps * sub).astype(F32)) * arriving_scr[p : p + 1, lanes]
            )
        for j in range(steps):
            if j % 2 == 0:
                both_rows = slice(j * SUBS, (j + 2) * SUBS)
                local = made_ref[0, both_rows, lanes].astype(F32)
                asked = made_ref[1, both_rows, lanes].astype(F32)
            half = slice((j % 2) * SUBS, (j % 2 + 1) * SUBS)
            out_scr[pl.ds(j, SUBS, stride=PITCH), :] = (
                local[half] + asked[half] * summed(fading)
            )
            fading = [d * f for d, f in zip(decay, fading)]
        for s in range(SUBS):
            gated_ref[s * steps : (s + 1) * steps, lanes] = out_scr[
                s * PITCH : s * PITCH + steps
            ].astype(BF16)
        if g % 2 == 1:
            both = slice((g - 1) * LANES, (g + 1) * LANES)
            gated_copies.append(
                pltpu.make_async_copy(
                    gated_ref.at[:, both], gated_hbm.at[:, both], gated_sems.at[g // 2]
                )
            )
            gated_copies[-1].start()
            if g == 1:
                copy.wait()
            part = jnp.dot(gated_ref[:, both], unembed_ref[both], preferred_element_type=F32)
            if g == 1:
                sum_scr[...] = part
            elif g < groups - 1:
                sum_scr[...] += part
            else:
                logits = (sum_scr[...] + part).astype(BF16)
                for i in range(logits_ref.shape[0]):
                    logits_ref[i] = logits[i * share : (i + 1) * share]
    for c in gated_copies:
        c.wait()


def loss_kernel(targets_ref, parts_ref, loss_ref):
    members, share, vocab = parts_ref.shape
    logits = parts_ref[0].astype(F32)
    for i in range(1, members):
        logits = logits + parts_ref[i].astype(F32)
    place = lax.axis_index("chan")
    first = place * share
    row = lax.broadcasted_iota(jnp.int32, (share, 1), 0)
    target = jnp.zeros((share, 1), jnp.int32)
    for t in range(share):
        target = jnp.where(row == t, targets_ref[first + t], target)
    peak = jnp.max(logits, axis=1, keepdims=True)
    total = jnp.sum(jnp.exp(logits - peak), axis=1, keepdims=True)
    ids = lax.broadcasted_iota(jnp.int32, logits.shape, 1)
    picked = jnp.sum(jnp.where(ids == target, logits, 0.0), axis=1, keepdims=True)
    loss = peak + jnp.log(total) - picked
    lines, wide = loss_ref.shape[1:]
    lane = lax.broadcasted_iota(jnp.int32, (share, wide), 1)
    mine = lane == lax.rem(first, wide) + lax.broadcasted_iota(jnp.int32, (share, wide), 0)
    line = jnp.sum(jnp.where(mine, loss, 0.0), axis=0, keepdims=True)
    at = lax.broadcasted_iota(jnp.int32, (lines, wide), 0) == lax.div(first, wide)
    placed = jnp.where(at, line, 0.0)
    for i in range(loss_ref.shape[0]):
        loss_ref[i] = placed


def in_vmem(count):
    return [pl.BlockSpec(memory_space=pltpu.VMEM)] * count


def in_hbm(count):
    return [pl.BlockSpec(memory_space=pltpu.HBM)] * count


def kept_in_hbm(*arrays):
    return [pltpu.with_memory_space_constraint(x, pltpu.HBM) for x in arrays]


def kept_in_vmem(*arrays):
    return [pltpu.with_memory_space_constraint(x, pltpu.VMEM) for x in arrays]


def in_smem(count):
    return [pl.BlockSpec(memory_space=pltpu.SMEM)] * count


PARAMS = pltpu.CompilerParams(vmem_limit_bytes=VMEM_LIMIT)


def local(row_members, streams, short_filter, pole_rates, residues, direct, doc_lengths, targets, unembed):
    block_len, chans = streams.shape[1:]
    poles = pole_rates.shape[0]
    vocab = unembed.shape[1]
    seq, chan = lax.axis_size("seq"), lax.axis_size("chan")
    rows = seq // row_members
    share = block_len // chan
    groups = chans // LANES
    halo = lax.ppermute(
        streams[:, block_len - 2 :, :], "seq", [(i, i + 1) for i in range(seq - 1)]
    )
    work = pl.pallas_call(
        first_kernel,
        out_shape=pltpu.VMEM((block_len + SUBS * (1 + poles), chans), F32),
        in_specs=in_hbm(4),
        out_specs=in_vmem(1)[0],
        scratch_shapes=[
            pltpu.SMEM(doc_lengths.shape, jnp.int32),
            pltpu.VMEM((2, block_len, chans), BF16),
            pltpu.VMEM(short_filter.shape, F32),
            pltpu.VMEM(pole_rates.shape, F32),
            pltpu.VMEM((block_len, LANES), F32),
            pltpu.VMEM((block_len, LANES), F32),
            pltpu.VMEM((2, SUBS * PITCH, LANES), F32),
            pltpu.SemaphoreType.DMA((3,)),
            pltpu.SemaphoreType.DMA((groups,)),
        ],
        compiler_params=PARAMS,
        cost_estimate=pl.CostEstimate(
            flops=60 * block_len * chans, bytes_accessed=4 * streams.size, transcendentals=0
        ),
        name="block_states",
    )(*kept_in_hbm(doc_lengths, streams, short_filter, pole_rates))
    ends = pl.pallas_call(
        functools.partial(join_kernel, block_len=block_len),
        out_shape=pltpu.VMEM((row_members, poles, chans), BF16),
        in_specs=in_smem(1) + in_vmem(5),
        out_specs=in_vmem(1)[0],
        scratch_shapes=[pltpu.VMEM((poles, chans), F32)] * 3,
        compiler_params=PARAMS,
        name="joined_states",
    )(doc_lengths, halo, short_filter, pole_rates, residues, *kept_in_vmem(work))
    along_row = [[r * row_members + i for i in range(row_members)] for r in range(rows)]
    across_rows = [[r * row_members + i for r in range(rows)] for i in range(row_members)]
    ends = lax.all_to_all(ends, "seq", 0, 0, axis_index_groups=along_row)
    totals = pl.pallas_call(
        functools.partial(row_kernel, block_len=block_len),
        out_shape=pltpu.VMEM((rows, poles, chans), BF16),
        in_specs=in_smem(1) + in_vmem(2),
        out_specs=in_vmem(1)[0],
        compiler_params=PARAMS,
        name="row_states",
    )(doc_lengths, pole_rates, ends)
    totals, work, halo = lax.optimization_barrier((totals, work, halo))
    totals = lax.all_to_all(totals, "seq", 0, 0, axis_index_groups=across_rows)
    made = pl.pallas_call(
        functools.partial(local_kernel, block_len=block_len),
        out_shape=pltpu.VMEM((2, block_len, chans), BF16),
        in_specs=in_smem(1) + in_vmem(2) + in_hbm(5),
        out_specs=in_vmem(1)[0],
        scratch_shapes=[
            pltpu.VMEM((block_len, chans), BF16),
            pltpu.VMEM(short_filter.shape, F32),
            pltpu.VMEM(pole_rates.shape, F32),
            pltpu.VMEM(residues.shape, F32),
            pltpu.VMEM((1, chans), F32),
            pltpu.VMEM((block_len, LANES), F32),
            pltpu.VMEM((block_len, LANES), F32),
            pltpu.VMEM((poles, chans), F32),
            pltpu.VMEM((poles, chans), F32),
            pltpu.VMEM((poles, chans), F32),
            pltpu.VMEM((2, chans), F32),
            pltpu.VMEM((SUBS * PITCH, LANES), F32),
            pltpu.VMEM((block_len, LANES), F32),
            pltpu.SemaphoreType.DMA((5,)),
        ],
        compiler_params=PARAMS,
        cost_estimate=pl.CostEstimate(
            flops=100 * block_len * chans, bytes_accessed=8 * streams.size, transcendentals=0
        ),
        name="local_out",
    )(
        doc_lengths, halo, *kept_in_vmem(work),
        *kept_in_hbm(streams, short_filter, pole_rates, residues, direct[None]),
    )
    gated, logits = pl.pallas_call(
        functools.partial(out_kernel, block_len=block_len, row_members=row_members),
        out_shape=(
            jax.ShapeDtypeStruct((block_len, chans), BF16),
            pltpu.VMEM((chan, share, vocab), BF16),
        ),
        in_specs=in_smem(1) + in_vmem(3) + in_hbm(1),
        out_specs=in_hbm(1) + in_vmem(1),
        scratch_shapes=[
            pltpu.VMEM(unembed.shape, BF16),
            pltpu.VMEM((block_len, chans), BF16),
            pltpu.VMEM((poles, chans), F32),
            pltpu.VMEM((SUBS * PITCH, LANES), F32),
            pltpu.VMEM((block_len, vocab), F32),
            pltpu.SemaphoreType.DMA,
            pltpu.SemaphoreType.DMA((groups // 2,)),
        ],
        compiler_params=PARAMS,
        name="gated_logits",
    )(doc_lengths, totals, pole_rates, *kept_in_vmem(made), *kept_in_hbm(unembed))
    parts = lax.all_to_all(logits, "chan", 0, 0)
    losses = pl.pallas_call(
        loss_kernel,
        out_shape=pltpu.VMEM((chan, block_len // LANES, LANES), F32),
        in_specs=in_smem(1) + in_vmem(1),
        out_specs=pl.BlockSpec(memory_space=pltpu.VMEM),
        compiler_params=PARAMS,
        name="token_losses",
    )(targets, parts)
    losses = lax.all_to_all(losses, "chan", 0, 0)
    return gated, jnp.sum(losses, axis=0).reshape(block_len)


def solution(mesh):
    seq = mesh.shape["seq"]
    row_members = 8 if seq % 8 == 0 else seq
    in_specs = (
        P(None, "seq", "chan"),
        P(None, None, "chan"),
        P(None, "chan"),
        P(None, "chan"),
        P("chan"),
        P(),
        P("seq"),
        P("chan", None),
    )
    out_specs = (P("seq", "chan"), P("seq"))
    return jax.shard_map(
        functools.partial(local, row_members),
        mesh=mesh,
        in_specs=in_specs,
        out_specs=out_specs,
        check_vma=False,
    )
```

time: 85.2 us -> 76.2 us (0.89)
  waiting for transfers between devices: 13.6 us -> 5.66 us
  Pallas kernels: 11 us -> 16.3 us
  starting transfers between devices: 12.2 us -> 7.13 us
  local copies, waits for them, and re-layouts: 5.69 us -> 0.85 us
  blocking collectives: 40.8 us -> 44.4 us
    pallas_call x2 -> x4, Pallas kernels: 5.14 us -> 11.2 us  [the longest x1 5.83 us: local(): pl.pallas_call(functools.partial(local_kernel, block_len=block_len), out_...]
    all_to_all x1, starting transfers between devices: 10.3 us -> 5.08 us  [local(): totals = lax.all_to_all(totals, 'seq', 0, 0, axis_index_groups=across_rows)]
    all_to_all x1, waiting for transfers between devices: 10.5 us -> 5.66 us  [local(): totals = lax.all_to_all(totals, 'seq', 0, 0, axis_index_groups=across_rows)]
    unnamed x16 -> x12, local copies, waits for them, and re-layouts: 3.72 us -> 0.04 us
    ppermute x1, waiting for transfers between devices: 3.08 us -> 0.01 us  [local(): lax.ppermute(streams[:, block_len - 2:, :], 'seq', [(i, i + 1) for i in r...]
    all_to_all x1, blocking collectives: 11.5 us -> 13.8 us  [local(): ends = lax.all_to_all(ends, 'seq', 0, 0, axis_index_groups=along_row)]
    pallas_call x1, Pallas kernels: 5.22 us -> 3.71 us  [local(): pl.pallas_call(functools.partial(out_kernel, block_len=block_len, row_mem...]
    all_to_all x1, blocking collectives: 19.3 us -> 20.6 us  [local(): parts = lax.all_to_all(logits, 'chan', 0, 0)]
  transfers between devices with their start and end apart: 2 -> 2, of which waited for: 2 -> 1; matrix products, arithmetic and copies ran while one was open for 0% -> 0% of each run, Pallas kernels for 0% -> 13%
where the time goes in v2:
time: 76.2 us; the launch traced here: 75.7 us
  blocking collectives  44.4 us (58%)
  Pallas kernels  16.3 us (21%)
  starting transfers between devices  7.13 us (9%)
  waiting for transfers between devices  5.66 us (7%)
  local copies, waits for them, and re-layouts  0.85 us (1%)
    all_to_all x1, blocking collectives, local(): parts = lax.all_to_all(logits, 'chan', 0, 0)  20.6 us
    all_to_all x1, blocking collectives, local(): ends = lax.all_to_all(ends, 'seq', 0, 0, axis_index_groups=along_row)  13.8 us
    all_to_all x1, blocking collectives, local(): losses = lax.all_to_all(losses, 'chan', 0, 0)  10.1 us
    pallas_call x1, Pallas kernels, local(): pl.pallas_call(functools.partial(local_kernel, block_len=block_len), out_...  5.83 us
    all_to_all x1, waiting for transfers between devices, local(): totals = lax.all_to_all(totals, 'seq', 0, 0, axis_index_groups=across_rows)  5.66 us
    all_to_all x1, starting transfers between devices, local(): totals = lax.all_to_all(totals, 'seq', 0, 0, axis_index_groups=across_rows)  5.08 us
    pallas_call x1, Pallas kernels, local(): pl.pallas_call(functools.partial(out_kernel, block_len=block_len, row_mem...  3.71 us
    pallas_call x1, Pallas kernels, local(): pl.pallas_call(first_kernel, out_shape=pltpu.VMEM((block_len + SUBS * (1...  3.64 us
  transfers between devices with their start and end apart: 2, of which 1 were waited for; matrix products, arithmetic and copies ran while one was open for 0% of the time, Pallas kernels for 13%

profile of v2, /device:TPU:2, one launch (start us, length us, event | category | flops | bytes accessed | tf_op | source)
XLA Modules:
  0.0 75.7 jit_solution(5817426089352445444)
XLA Ops:
  0.6 0.8 %slice.3 = bf16[3,2,1024]{2,1,0:T(2,128)(2,1)S(1)} slice(bf16[3,256,1024]{2,1,0:T(8,128)(2,1)} %streams_hbm.3), slice={[0:3], [254:256], [0:1024]} | slice | bytes 24576 | tf_op jit(solution)/shard_map/slice | solution.py:484
  1.4 0.0 copy-start
  1.5 0.0 copy-start.2
  1.5 0.0 copy-start.3
  1.5 0.0 copy-start.4
  1.5 2.1 %collective-permute-start = (bf16[3,2,1024]{2,1,0:T(2,128)(2,1)S(1)}, bf16[3,2,1024]{2,1,0:T(2,128)(2,1)S(1)}, u32[]{:S(2)}, u32[]{:S(2)}) collective-permute-start(bf16[3,2,1024]{2,1,0:T(2,128)(2,1)S(1)} %slice.3), channel_id=1, source_target_pairs={{0,8},{8,16},{16,24},{24,32},{32,40},{40,48},{48,56},{56,64},{64,7... | collective-permute-start | bytes 36872 | tf_op jit(solution)/shard_map/ppermute | solution.py:483
  3.6 3.6 %block_states.1.work_ref = f32[392,1024]{1,0:T(8,128)S(1)} custom-call(s32[4]{0:T(128)} %docs_ref.7, bf16[3,256,1024]{2,1,0:T(8,128)(2,1)} %streams_hbm.3, f32[3,3,1024]{2,1,0:T(4,128)} %taps_hbm.3, f32[16,1024]{1,0:T(8,128)} %rates_ref.5), custom_call_target="tpu_custom_call" | custom-call | flops 15728640 | bytes 3145728 | tf_op jit(solution)/shard_map/block_states/pallas_call | solution.py:486
  7.2 0.0 collective-permute-done.halo_ref
  7.2 0.0 copy-done
  7.2 0.0 copy-done.2
  7.2 0.0 copy-done.3
  7.2 0.0 copy-done.4
  7.3 0.9 %joined_states.1 = bf16[8,16,1024]{2,1,0:T(8,128)(2,1)S(1)} custom-call(s32[4]{0:T(128)S(1)} %copy-done.4, bf16[3,2,1024]{2,1,0:T(2,128)(2,1)S(1)} %collective-permute-done.halo_ref, f32[3,3,1024]{2,1,0:T(4,128)S(1)} %copy-done.2, f32[16,1024]{1,0:T(8,128)S(1)} %copy-done, f32[16,1024]{1,0:T(8,128)S(1)} %copy-done.3, f32[392,1024]{1,0:T(8,128)S(1)} %block_states.1.work_ref), custom_call_target="tpu_custom_call" | custom-call | tf_op jit(solution)/shard_map/joined_states/pallas_call | solution.py:508
  8.2 13.8 %all_to_all.20.ends_ref = bf16[8,16,1024]{2,1,0:T(8,128)(2,1)S(1)} all-to-all(bf16[8,16,1024]{2,1,0:T(8,128)(2,1)S(1)} %joined_states.1), channel_id=1, replica_groups={{0,8,16,24,32,40,48,56},{64,72,80,88,96,104,112,120},{128,136,144,152,1..., dimensions={0} | all-to-all | bytes 524288 | tf_op jit(solution)/shard_map/all_to_all | solution.py:519
  22.0 1.4 %row_states.1 = bf16[8,16,1024]{2,1,0:T(8,128)(2,1)} custom-call(s32[4]{0:T(128)S(1)} %copy-done.4, f32[16,1024]{1,0:T(8,128)S(1)} %copy-done, bf16[8,16,1024]{2,1,0:T(8,128)(2,1)S(1)} %all_to_all.20.ends_ref), custom_call_target="tpu_custom_call" | custom-call | tf_op jit(solution)/shard_map/row_states/pallas_call | solution.py:520
  23.3 5.1 %all-to-all-start.1 = ((bf16[8,16,1024]{2,1,0:T(8,128)(2,1)}), bf16[8,16,1024]{2,1,0:T(8,128)(2,1)S(1)}, u32[]{:S(2)}, u32[]{:S(2)}) async-start(bf16[8,16,1024]{2,1,0:T(8,128)(2,1)} %row_states.1), calls=%async_computation.1 | async-start | bytes 524288 | tf_op jit(solution)/shard_map/all_to_all | solution.py:529
  28.4 0.0 copy-start.1
  28.4 5.8 %local_out.1.made_ref = bf16[2,256,1024]{2,1,0:T(8,128)(2,1)S(1)} custom-call(s32[4]{0:T(128)S(1)} %copy-done.4, bf16[3,2,1024]{2,1,0:T(2,128)(2,1)S(1)} %collective-permute-done.halo_ref, f32[392,1024]{1,0:T(8,128)S(1)} %block_states.1.work_ref, bf16[3,256,1024]{2,1,0:T(8,128)(2,1)} %streams_hbm.3, f32[3,3,1024]{2,1,0:T(4,128)} %taps_hbm.3, ...), custom_call_target="tpu_custom_call" | custom-call | flops 26214400 | bytes 6291456 | tf_op jit(solution)/shard_map/local_out/pallas_call | solution.py:530
  34.3 0.0 copy-start.5
  34.3 5.7 %all-to-all-done.1.totals_ref = bf16[8,16,1024]{2,1,0:T(8,128)(2,1)S(1)} async-done(((bf16[8,16,1024]{2,1,0:T(8,128)(2,1)}), bf16[8,16,1024]{2,1,0:T(8,128)(2,1)S(1)}, u32[]{:S(2)}, u32[]{:S(2)}) %all-to-all-start.1) | async-done | bytes 262176 | tf_op jit(solution)/shard_map/all_to_all | solution.py:529
  39.9 0.0 copy-done.1
  39.9 3.7 %gated_logits.1 = (bf16[256,1024]{1,0:T(8,128)(2,1)}, bf16[8,32,512]{2,1,0:T(8,128)(2,1)S(1)}) custom-call(s32[4]{0:T(128)S(1)} %copy-done.4, bf16[8,16,1024]{2,1,0:T(8,128)(2,1)S(1)} %all-to-all-done.1.totals_ref, f32[16,1024]{1,0:T(8,128)S(1)} %copy-done.1, bf16[2,256,1024]{2,1,0:T(8,128)(2,1)S(1)} %local_out.1.made_ref, bf16[1024,512]{1,0:T(8,128)(2,1)} %unembed_hbm.1), custom_call_target="tpu_custom_call" | custom-call | tf_op jit(solution)/shard_map/gated_logits/pallas_call | solution.py:560
  43.7 20.6 %all_to_all.21.parts_ref = bf16[8,32,512]{2,1,0:T(8,128)(2,1)S(1)} all-to-all(bf16[8,32,512]{2,1,0:T(8,128)(2,1)S(1)} %get-tuple-element.11), channel_id=1, replica_groups=mesh['seq'=64,'chan'=8] {'chan'}, dimensions={0} | all-to-all | bytes 524288 | tf_op jit(solution)/shard_map/all_to_all | solution.py:580
  64.3 0.0 copy-done.5
  64.3 0.8 %token_losses.1 = f32[8,2,128]{2,1,0:T(2,128)S(1)} custom-call(s32[256]{0:T(256)S(1)} %copy-done.5, bf16[8,32,512]{2,1,0:T(8,128)(2,1)S(1)} %all_to_all.21.parts_ref), custom_call_target="tpu_custom_call" | custom-call | tf_op jit(solution)/shard_map/token_losses/pallas_call | solution.py:581
  65.0 10.1 %all_to_all.22 = f32[8,2,128]{2,1,0:T(2,128)S(1)} all-to-all(f32[8,2,128]{2,1,0:T(2,128)S(1)} %token_losses.1), channel_id=1, replica_groups=mesh['seq'=64,'chan'=8] {'chan'}, dimensions={0} | all-to-all | bytes 16384 | tf_op jit(solution)/shard_map/all_to_all | solution.py:589
  75.1 0.6 reduce_sum.9
Async XLA Ops:
  1.4 5.8 %copy-start = (f32[16,1024]{1,0:T(8,128)S(1)}, f32[16,1024]{1,0:T(8,128)}, u32[]{:S(2)}) copy-start(f32[16,1024]{1,0:T(8,128)} %rates_ref.5) | copy-start | bytes 196612
  1.5 5.8 %copy-start.2 = (f32[3,3,1024]{2,1,0:T(4,128)S(1)}, f32[3,3,1024]{2,1,0:T(4,128)}, u32[]{:S(2)}) copy-start(f32[3,3,1024]{2,1,0:T(4,128)} %taps_hbm.3) | copy-start | bytes 110596
  1.5 5.8 %copy-start.3 = (f32[16,1024]{1,0:T(8,128)S(1)}, f32[16,1024]{1,0:T(8,128)}, u32[]{:S(2)}) copy-start(f32[16,1024]{1,0:T(8,128)} %residues_hbm.1) | copy-start | bytes 196612
  1.5 5.8 %copy-start.4 = (s32[4]{0:T(128)S(1)}, s32[4]{0:T(128)}, u32[]{:S(2)}) copy-start(s32[4]{0:T(128)} %docs_ref.7) | copy-start | bytes 52
  1.5 5.7 %collective-permute-start = (bf16[3,2,1024]{2,1,0:T(2,128)(2,1)S(1)}, bf16[3,2,1024]{2,1,0:T(2,128)(2,1)S(1)}, u32[]{:S(2)}, u32[]{:S(2)}) collective-permute-start(bf16[3,2,1024]{2,1,0:T(2,128)(2,1)S(1)} %slice.3), channel_id=1, source_target_pairs={{0,8},{8,16},{16,24},{24,32},{32,40},{40,48},{48,56},{56,64},{64,7... | collective-permute-start | bytes 36872 | tf_op jit(solution)/shard_map/ppermute | solution.py:483
  23.3 16.6 %all-to-all-start.1 = ((bf16[8,16,1024]{2,1,0:T(8,128)(2,1)}), bf16[8,16,1024]{2,1,0:T(8,128)(2,1)S(1)}, u32[]{:S(2)}, u32[]{:S(2)}) async-start(bf16[8,16,1024]{2,1,0:T(8,128)(2,1)} %row_states.1), calls=%async_computation.1 | async-start | bytes 524288 | tf_op jit(solution)/shard_map/all_to_all | solution.py:529
  28.4 11.5 %copy-start.1 = (f32[16,1024]{1,0:T(8,128)S(1)}, f32[16,1024]{1,0:T(8,128)}, u32[]{:S(2)}) copy-start(f32[16,1024]{1,0:T(8,128)} %rates_ref.5) | copy-start | bytes 196612
  34.3 30.0 %copy-start.5 = (s32[256]{0:T(256)S(1)}, s32[256]{0:T(256)}, u32[]{:S(2)}) copy-start(s32[256]{0:T(256)} %targets_ref.1) | copy-start | bytes 3076

commit v3 on v2

--- a/solution.py
+++ b/solution.py
@@ -124,27 +124,33 @@
         for j, (key, value) in enumerate(zip(steps_of(0), steps_of(1))):
             rows = slice(j * SUBS, (j + 1) * SUBS)
             if j < 2:
-                work_ref[block_len + j : block_len + 1 + j, lanes] = key[0:1]
-                work_ref[block_len + 2 + j : block_len + 3 + j, lanes] = value[0:1]
+                work_ref[g, block_len + j : block_len + 1 + j] = key[0:1]
+                work_ref[g, block_len + 2 + j : block_len + 3 + j] = value[0:1]
             driver = key * value
-            work_ref[rows, lanes] = driver
+            work_ref[g, rows] = driver
             masked = driver * tail_scr[rows]
             state = [d * s + masked for d, s in zip(decay, state)]
         for p in range(poles):
             at = block_len + SUBS * (1 + p)
-            work_ref[at : at + SUBS, lanes] = state[p]
+            work_ref[g, at : at + SUBS] = state[p]
         return carry
 
     lax.fori_loop(0, groups, group, 0)
 
 
-def corrected(starts, first, steps, halo_ref, taps_ref, edge):
+def edge_marks(starts, first, steps):
     older = no_start_in(starts, first - 1, first)
     keep = [no_start_in(starts, first + j, first + j + 1) for j in range(2)]
+    counts = [no_start_in(starts, first + j + 1, first + steps) for j in range(2)]
+    return older, keep, counts
+
+
+def corrected(marks, halo_ref, taps_ref, edge, lanes):
+    older, keep, counts = marks
 
     def added(i):
-        halo = halo_ref[i].astype(F32)
-        taps = taps_ref[i]
+        halo = halo_ref[i, :, lanes].astype(F32)
+        taps = taps_ref[i, :, lanes]
         near = (keep[0] * taps[1:2]) * halo[1:2] + (keep[0] * older * taps[2:3]) * halo[0:1]
         return near, (keep[1] * keep[0] * taps[2:3]) * halo[1:2]
 
@@ -153,9 +159,8 @@
     for j in range(2):
         old_key, old_value = edge[j : j + 1], edge[2 + j : 3 + j]
         driver = (old_key + key[j]) * (old_value + value[j])
-        counts = no_start_in(starts, first + j + 1, first + steps)
         drivers.append(driver)
-        changes.append(counts * (driver - old_key * old_value))
+        changes.append(counts[j] * (driver - old_key * old_value))
     return drivers, changes
 
 
@@ -182,35 +187,31 @@
 
 
 def join_kernel(
-    docs_ref, halo_ref, taps_ref, rates_ref, residues_ref, work_ref,
-    ends_ref, old_scr, young_scr, end_scr,
-    *, block_len,
+    docs_ref, halo_ref, taps_ref, rates_ref, residues_ref, work_ref, ends_ref, *, block_len
 ):
     poles, chans = rates_ref.shape
     steps = block_len // SUBS
     first = lax.axis_index("seq") * block_len
     starts = start_positions(docs_ref, docs_ref.shape[0])
-    edge = work_ref[block_len : block_len + SUBS]
-    _, changes = corrected(starts, first, steps, halo_ref, taps_ref, edge)
-    rates = rates_ref[...]
-    young_scr[...] = jnp.exp(-rates * (steps - 1)) * changes[0] + jnp.exp(-rates * (steps - 2)) * changes[1]
-    old_scr[...] = jnp.exp(-rates * steps)
-    reach = chunk_reach(starts, first, steps)
+    marks = edge_marks(starts, first, steps)
+    clean = [
+        no_start_in(starts, first + s * steps, first + (s + 1) * steps) for s in range(SUBS)
+    ]
     for g in range(chans // LANES):
         lanes = slice(g * LANES, (g + 1) * LANES)
-        for p in range(poles):
-            at = block_len + SUBS * (1 + p)
-            total = chunk_ends(
-                work_ref[at : at + SUBS, lanes],
-                young_scr[p : p + 1, lanes],
-                old_scr[p : p + 1, lanes],
-                reach,
-            )
-            end_scr[p : p + 1, lanes] = total[SUBS - 1 : SUBS]
-    decays = jnp.exp(-rates)
-    ends = (residues_ref[...] * ((1.0 - decays) * decays) * end_scr[...]).astype(BF16)
-    for i in range(ends_ref.shape[0]):
-        ends_ref[i] = ends
+        edge = work_ref[g, block_len : block_len + SUBS]
+        _, changes = corrected(marks, halo_ref, taps_ref, edge, lanes)
+        rates = rates_ref[:, lanes]
+        decays = jnp.exp(-rates)
+        transfer = jnp.exp(-rates * steps)
+        total = jnp.exp(-rates * (steps - 2)) * (decays * changes[0] + changes[1])
+        for s in range(SUBS):
+            if s > 0:
+                total = (transfer * clean[s]) * total
+            total = total + work_ref[g, pl.ds(block_len + SUBS + s, poles, stride=SUBS), :]
+        ends = (residues_ref[:, lanes] * ((1.0 - decays) * decays) * total).astype(BF16)
+        for i in range(ends_ref.shape[0]):
+            ends_ref[i, :, lanes] = ends
 
 
 def row_kernel(docs_ref, rates_ref, ends_ref, totals_ref, *, block_len):
@@ -228,8 +229,10 @@
         low = row_first + j * block_len
         total = (transfer * no_start_in(starts, low, low + block_len)) * total + ends_ref[j].astype(F32)
     row = lax.div(block, members)
+    rounded = total.astype(BF16)
     for i in range(totals_ref.shape[0]):
-        totals_ref[i] = jnp.where(row == i, before, total).astype(BF16)
+        totals_ref[i] = rounded
+    totals_ref[row] = before.astype(BF16)
 
 
 def local_kernel(
@@ -270,15 +273,19 @@
     reach = chunk_reach(starts, first, steps)
     for c in copies:
         c.wait()
-    edge = work_ref[block_len : block_len + SUBS]
-    drivers, changes = corrected(starts, first, steps, halo_ref, taps_ref, edge)
     rates = rates_ref[...]
     decays = jnp.exp(-rates)
     weight_scr[...] = residues_ref[...] * (1.0 - decays)
-    young_scr[...] = jnp.exp(-rates * (steps - 1)) * changes[0] + jnp.exp(-rates * (steps - 2)) * changes[1]
+    older = jnp.exp(-rates * (steps - 2))
     old_scr[...] = jnp.exp(-rates * steps)
-    for j in range(2):
-        first_scr[j : j + 1] = drivers[j]
+    marks = edge_marks(starts, first, steps)
+    for g in range(chans // LANES):
+        lanes = slice(g * LANES, (g + 1) * LANES)
+        edge = work_ref[g, block_len : block_len + SUBS]
+        drivers, changes = corrected(marks, halo_ref, taps_ref, edge, lanes)
+        young_scr[:, lanes] = older[:, lanes] * (decays[:, lanes] * changes[0] + changes[1])
+        for j in range(2):
+            first_scr[j : j + 1, lanes] = drivers[j]
 
     def group(g, carry):
         lanes = pl.ds(pl.multiple_of(g * LANES, LANES), LANES)
@@ -293,7 +300,7 @@
             weight.append(jnp.broadcast_to(weight_scr[p : p + 1, lanes], (SUBS, LANES)))
             at = block_len + SUBS * (1 + p)
             total = chunk_ends(
-                work_ref[at : at + SUBS, lanes],
+                work_ref[g, at : at + SUBS],
                 young_scr[p : p + 1, lanes],
                 old_scr[p : p + 1, lanes],
                 reach,
@@ -302,7 +309,7 @@
         direct = jnp.broadcast_to(direct_ref[0:1, lanes], (SUBS, LANES))
         for j in range(steps):
             rows = slice(j * SUBS, (j + 1) * SUBS)
-            driver = work_ref[rows, lanes]
+            driver = work_ref[g, rows]
             if j < 2:
                 driver = jnp.where(sub == 0, first_scr[j : j + 1, lanes], driver)
             keep = keep_scr[rows]
@@ -344,7 +351,7 @@
 def out_kernel(
     docs_ref, totals_ref, rates_ref, made_ref, unembed_hbm,
     gated_hbm, logits_ref,
-    unembed_ref, gated_ref, arriving_scr, out_scr, sum_scr, sem, gated_sems,
+    unembed_ref, gated_ref, arriving_scr, out_scr, sem, gated_sems,
     *, block_len, row_members,
 ):
     poles, chans = rates_ref.shape
@@ -408,17 +415,10 @@
                 )
             )
             gated_copies[-1].start()
-            if g == 1:
-                copy.wait()
-            part = jnp.dot(gated_ref[:, both], unembed_ref[both], preferred_element_type=F32)
-            if g == 1:
-                sum_scr[...] = part
-            elif g < groups - 1:
-                sum_scr[...] += part
-            else:
-                logits = (sum_scr[...] + part).astype(BF16)
-                for i in range(logits_ref.shape[0]):
-                    logits_ref[i] = logits[i * share : (i + 1) * share]
+    copy.wait()
+    logits = jnp.dot(gated_ref[...], unembed_ref[...], preferred_element_type=F32).astype(BF16)
+    for i in range(logits_ref.shape[0]):
+        logits_ref[i] = logits[i * share : (i + 1) * share]
     for c in gated_copies:
         c.wait()
 
@@ -485,7 +485,7 @@
     )
     work = pl.pallas_call(
         first_kernel,
-        out_shape=pltpu.VMEM((block_len + SUBS * (1 + poles), chans), F32),
+        out_shape=pltpu.VMEM((groups, block_len + SUBS * (1 + poles), LANES), F32),
         in_specs=in_hbm(4),
         out_specs=in_vmem(1)[0],
         scratch_shapes=[
@@ -510,7 +510,6 @@
         out_shape=pltpu.VMEM((row_members, poles, chans), BF16),
         in_specs=in_smem(1) + in_vmem(5),
         out_specs=in_vmem(1)[0],
-        scratch_shapes=[pltpu.VMEM((poles, chans), F32)] * 3,
         compiler_params=PARAMS,
         name="joined_states",
     )(doc_lengths, halo, short_filter, pole_rates, residues, *kept_in_vmem(work))
@@ -570,7 +569,6 @@
             pltpu.VMEM((block_len, chans), BF16),
             pltpu.VMEM((poles, chans), F32),
             pltpu.VMEM((SUBS * PITCH, LANES), F32),
-            pltpu.VMEM((block_len, vocab), F32),
             pltpu.SemaphoreType.DMA,
             pltpu.SemaphoreType.DMA((groups // 2,)),
         ],

time: 76.2 us -> 75.1 us (0.986)
  Pallas kernels: 16.3 us -> 15.2 us
    pallas_call x1, Pallas kernels: 3.71 us -> 2.81 us  [local(): pl.pallas_call(functools.partial(out_kernel, block_len=block_len, row_mem...]
where the time goes in v3:
time: 75.1 us; the launch traced here: 74.6 us
  blocking collectives  44.4 us (59%)
  Pallas kernels  15.2 us (20%)
  starting transfers between devices  7.16 us (10%)
  waiting for transfers between devices  5.65 us (8%)
  local copies, waits for them, and re-layouts  0.85 us (1%)
  between operations  0.76 us (1%)
    all_to_all x1, blocking collectives, local(): parts = lax.all_to_all(logits, 'chan', 0, 0)  20.6 us
    all_to_all x1, blocking collectives, local(): ends = lax.all_to_all(ends, 'seq', 0, 0, axis_index_groups=along_row)  13.8 us
    all_to_all x1, blocking collectives, local(): losses = lax.all_to_all(losses, 'chan', 0, 0)  10.1 us
    pallas_call x1, Pallas kernels, local(): pl.pallas_call(functools.partial(local_kernel, block_len=block_len), out_...  5.83 us
    all_to_all x1, waiting for transfers between devices, local(): totals = lax.all_to_all(totals, 'seq', 0, 0, axis_index_groups=across_rows)  5.65 us
    all_to_all x1, starting transfers between devices, local(): totals = lax.all_to_all(totals, 'seq', 0, 0, axis_index_groups=across_rows)  5.1 us
    pallas_call x1, Pallas kernels, local(): pl.pallas_call(first_kernel, out_shape=pltpu.VMEM((groups, block_len + SU...  3.62 us
    pallas_call x1, Pallas kernels, local(): pl.pallas_call(functools.partial(out_kernel, block_len=block_len, row_mem...  2.81 us
  transfers between devices with their start and end apart: 2, of which 1 were waited for; matrix products, arithmetic and copies ran while one was open for 0% of the time, Pallas kernels for 13%

profile of v3, /device:TPU:2, one launch (start us, length us, event | category | flops | bytes accessed | tf_op | source)
XLA Modules:
  0.0 74.6 jit_solution(10253884990923463189)
XLA Ops:
  0.6 0.8 %slice.3 = bf16[3,2,1024]{2,1,0:T(2,128)(2,1)S(1)} slice(bf16[3,256,1024]{2,1,0:T(8,128)(2,1)} %streams_hbm.3), slice={[0:3], [254:256], [0:1024]} | slice | bytes 24576 | tf_op jit(solution)/shard_map/slice | solution.py:484
  1.4 0.0 copy-start
  1.5 0.0 copy-start.2
  1.5 0.0 copy-start.3
  1.5 0.0 copy-start.4
  1.5 2.1 %collective-permute-start = (bf16[3,2,1024]{2,1,0:T(2,128)(2,1)S(1)}, bf16[3,2,1024]{2,1,0:T(2,128)(2,1)S(1)}, u32[]{:S(2)}, u32[]{:S(2)}) collective-permute-start(bf16[3,2,1024]{2,1,0:T(2,128)(2,1)S(1)} %slice.3), channel_id=1, source_target_pairs={{0,8},{8,16},{16,24},{24,32},{32,40},{40,48},{48,56},{56,64},{64,7... | collective-permute-start | bytes 36872 | tf_op jit(solution)/shard_map/ppermute | solution.py:483
  3.6 3.6 %block_states.1.work_ref = f32[8,392,128]{2,1,0:T(8,128)S(1)} custom-call(s32[4]{0:T(128)} %docs_ref.7, bf16[3,256,1024]{2,1,0:T(8,128)(2,1)} %streams_hbm.3, f32[3,3,1024]{2,1,0:T(4,128)} %taps_hbm.3, f32[16,1024]{1,0:T(8,128)} %rates_ref.5), custom_call_target="tpu_custom_call" | custom-call | flops 15728640 | bytes 3145728 | tf_op jit(solution)/shard_map/block_states/pallas_call | solution.py:486
  7.2 0.0 collective-permute-done.halo_ref
  7.2 0.0 copy-done
  7.2 0.0 copy-done.2
  7.2 0.0 copy-done.3
  7.2 0.0 copy-done.4
  7.2 0.8 %joined_states.1 = bf16[8,16,1024]{2,1,0:T(8,128)(2,1)S(1)} custom-call(s32[4]{0:T(128)S(1)} %copy-done.4, bf16[3,2,1024]{2,1,0:T(2,128)(2,1)S(1)} %collective-permute-done.halo_ref, f32[3,3,1024]{2,1,0:T(4,128)S(1)} %copy-done.2, f32[16,1024]{1,0:T(8,128)S(1)} %copy-done, f32[16,1024]{1,0:T(8,128)S(1)} %copy-done.3, f32[8,392,128]{2,1,0:T(8,128)S(1)} %block_states.1.work_ref), custom_call_target="tpu_custom_call" | custom-call | tf_op jit(solution)/shard_map/joined_states/pallas_call | solution.py:508
  8.0 13.8 %all_to_all.20.ends_ref = bf16[8,16,1024]{2,1,0:T(8,128)(2,1)S(1)} all-to-all(bf16[8,16,1024]{2,1,0:T(8,128)(2,1)S(1)} %joined_states.1), channel_id=1, replica_groups={{0,8,16,24,32,40,48,56},{64,72,80,88,96,104,112,120},{128,136,144,152,1..., dimensions={0} | all-to-all | bytes 524288 | tf_op jit(solution)/shard_map/all_to_all | solution.py:518
  21.8 1.4 %row_states.1 = bf16[8,16,1024]{2,1,0:T(8,128)(2,1)} custom-call(s32[4]{0:T(128)S(1)} %copy-done.4, f32[16,1024]{1,0:T(8,128)S(1)} %copy-done, bf16[8,16,1024]{2,1,0:T(8,128)(2,1)S(1)} %all_to_all.20.ends_ref), custom_call_target="tpu_custom_call" | custom-call | tf_op jit(solution)/shard_map/row_states/pallas_call | solution.py:519
  23.2 5.1 %all-to-all-start.1 = ((bf16[8,16,1024]{2,1,0:T(8,128)(2,1)}), bf16[8,16,1024]{2,1,0:T(8,128)(2,1)S(1)}, u32[]{:S(2)}, u32[]{:S(2)}) async-start(bf16[8,16,1024]{2,1,0:T(8,128)(2,1)} %row_states.1), calls=%async_computation.1 | async-start | bytes 524288 | tf_op jit(solution)/shard_map/all_to_all | solution.py:528
  28.3 0.0 copy-start.1
  28.3 5.8 %local_out.1.made_ref = bf16[2,256,1024]{2,1,0:T(8,128)(2,1)S(1)} custom-call(s32[4]{0:T(128)S(1)} %copy-done.4, bf16[3,2,1024]{2,1,0:T(2,128)(2,1)S(1)} %collective-permute-done.halo_ref, f32[8,392,128]{2,1,0:T(8,128)S(1)} %block_states.1.work_ref, bf16[3,256,1024]{2,1,0:T(8,128)(2,1)} %streams_hbm.3, f32[3,3,1024]{2,1,0:T(4,128)} %taps_hbm.3, ...), custom_call_target="tpu_custom_call" | custom-call | flops 26214400 | bytes 6291456 | tf_op jit(solution)/shard_map/local_out/pallas_call | solution.py:529
  34.1 0.0 copy-start.5
  34.1 5.7 %all-to-all-done.1.totals_ref = bf16[8,16,1024]{2,1,0:T(8,128)(2,1)S(1)} async-done(((bf16[8,16,1024]{2,1,0:T(8,128)(2,1)}), bf16[8,16,1024]{2,1,0:T(8,128)(2,1)S(1)}, u32[]{:S(2)}, u32[]{:S(2)}) %all-to-all-start.1) | async-done | bytes 262176 | tf_op jit(solution)/shard_map/all_to_all | solution.py:528
  39.8 0.0 copy-done.1
  39.8 2.8 %gated_logits.1 = (bf16[256,1024]{1,0:T(8,128)(2,1)}, bf16[8,32,512]{2,1,0:T(8,128)(2,1)S(1)}) custom-call(s32[4]{0:T(128)S(1)} %copy-done.4, bf16[8,16,1024]{2,1,0:T(8,128)(2,1)S(1)} %all-to-all-done.1.totals_ref, f32[16,1024]{1,0:T(8,128)S(1)} %copy-done.1, bf16[2,256,1024]{2,1,0:T(8,128)(2,1)S(1)} %local_out.1.made_ref, bf16[1024,512]{1,0:T(8,128)(2,1)} %unembed_hbm.1), custom_call_target="tpu_custom_call" | custom-call | tf_op jit(solution)/shard_map/gated_logits/pallas_call | solution.py:559
  42.6 20.6 %all_to_all.21.parts_ref = bf16[8,32,512]{2,1,0:T(8,128)(2,1)S(1)} all-to-all(bf16[8,32,512]{2,1,0:T(8,128)(2,1)S(1)} %get-tuple-element.11), channel_id=1, replica_groups=mesh['seq'=64,'chan'=8] {'chan'}, dimensions={0} | all-to-all | bytes 524288 | tf_op jit(solution)/shard_map/all_to_all | solution.py:578
  63.2 0.0 copy-done.5
  63.2 0.8 %token_losses.1 = f32[8,2,128]{2,1,0:T(2,128)S(1)} custom-call(s32[256]{0:T(256)S(1)} %copy-done.5, bf16[8,32,512]{2,1,0:T(8,128)(2,1)S(1)} %all_to_all.21.parts_ref), custom_call_target="tpu_custom_call" | custom-call | tf_op jit(solution)/shard_map/token_losses/pallas_call | solution.py:579
  64.0 10.1 %all_to_all.22 = f32[8,2,128]{2,1,0:T(2,128)S(1)} all-to-all(f32[8,2,128]{2,1,0:T(2,128)S(1)} %token_losses.1), channel_id=1, replica_groups=mesh['seq'=64,'chan'=8] {'chan'}, dimensions={0} | all-to-all | bytes 16384 | tf_op jit(solution)/shard_map/all_to_all | solution.py:587
  74.1 0.6 reduce_sum.9
Async XLA Ops:
  1.4 5.8 %copy-start = (f32[16,1024]{1,0:T(8,128)S(1)}, f32[16,1024]{1,0:T(8,128)}, u32[]{:S(2)}) copy-start(f32[16,1024]{1,0:T(8,128)} %rates_ref.5) | copy-start | bytes 196612
  1.5 5.7 %copy-start.2 = (f32[3,3,1024]{2,1,0:T(4,128)S(1)}, f32[3,3,1024]{2,1,0:T(4,128)}, u32[]{:S(2)}) copy-start(f32[3,3,1024]{2,1,0:T(4,128)} %taps_hbm.3) | copy-start | bytes 110596
  1.5 5.7 %copy-start.3 = (f32[16,1024]{1,0:T(8,128)S(1)}, f32[16,1024]{1,0:T(8,128)}, u32[]{:S(2)}) copy-start(f32[16,1024]{1,0:T(8,128)} %residues_hbm.1) | copy-start | bytes 196612
  1.5 5.7 %copy-start.4 = (s32[4]{0:T(128)S(1)}, s32[4]{0:T(128)}, u32[]{:S(2)}) copy-start(s32[4]{0:T(128)} %docs_ref.7) | copy-start | bytes 52
  1.5 5.7 %collective-permute-start = (bf16[3,2,1024]{2,1,0:T(2,128)(2,1)S(1)}, bf16[3,2,1024]{2,1,0:T(2,128)(2,1)S(1)}, u32[]{:S(2)}, u32[]{:S(2)}) collective-permute-start(bf16[3,2,1024]{2,1,0:T(2,128)(2,1)S(1)} %slice.3), channel_id=1, source_target_pairs={{0,8},{8,16},{16,24},{24,32},{32,40},{40,48},{48,56},{56,64},{64,7... | collective-permute-start | bytes 36872 | tf_op jit(solution)/shard_map/ppermute | solution.py:483
  23.2 16.6 %all-to-all-start.1 = ((bf16[8,16,1024]{2,1,0:T(8,128)(2,1)}), bf16[8,16,1024]{2,1,0:T(8,128)(2,1)S(1)}, u32[]{:S(2)}, u32[]{:S(2)}) async-start(bf16[8,16,1024]{2,1,0:T(8,128)(2,1)} %row_states.1), calls=%async_computation.1 | async-start | bytes 524288 | tf_op jit(solution)/shard_map/all_to_all | solution.py:528
  28.3 11.5 %copy-start.1 = (f32[16,1024]{1,0:T(8,128)S(1)}, f32[16,1024]{1,0:T(8,128)}, u32[]{:S(2)}) copy-start(f32[16,1024]{1,0:T(8,128)} %rates_ref.5) | copy-start | bytes 196612
  34.1 29.1 %copy-start.5 = (s32[256]{0:T(256)S(1)}, s32[256]{0:T(256)}, u32[]{:S(2)}) copy-start(s32[256]{0:T(256)} %targets_ref.1) | copy-start | bytes 3076

commit v4 on v3

--- a/solution.py
+++ b/solution.py
@@ -12,6 +12,7 @@
 LANES = 128
 SUBS = 8
 PITCH = 40
+LONGEST = 8192
 VMEM_LIMIT = 16 * 1024 * 1024
 
 
@@ -214,7 +215,7 @@
             ends_ref[i, :, lanes] = ends
 
 
-def row_kernel(docs_ref, rates_ref, ends_ref, totals_ref, *, block_len):
+def row_kernel(docs_ref, rates_ref, ends_ref, total_ref, before_ref, *, block_len):
     members = ends_ref.shape[0]
     block = lax.axis_index("seq")
     first = block * block_len
@@ -228,18 +229,15 @@
         before = jnp.where(me == j, total, before)
         low = row_first + j * block_len
         total = (transfer * no_start_in(starts, low, low + block_len)) * total + ends_ref[j].astype(F32)
-    row = lax.div(block, members)
-    rounded = total.astype(BF16)
-    for i in range(totals_ref.shape[0]):
-        totals_ref[i] = rounded
-    totals_ref[row] = before.astype(BF16)
+    total_ref[...] = total.astype(BF16)
+    before_ref[...] = before
 
 
 def local_kernel(
-    docs_ref, halo_ref, work_ref, streams_hbm, taps_hbm, rates_hbm, residues_hbm, direct_hbm,
-    made_ref,
-    stream_ref, taps_ref, rates_ref, residues_ref, direct_ref,
-    keep_scr, alive_scr, weight_scr, old_scr, young_scr, first_scr, wide_scr, local_scr, sems,
+    docs_ref, halo_ref, work_ref, taps_hbm, rates_hbm, residues_hbm, direct_hbm,
+    local_ref,
+    taps_ref, rates_ref, residues_ref, direct_ref,
+    keep_scr, weight_scr, old_scr, young_scr, first_scr, sems,
     *, block_len,
 ):
     poles, chans = rates_ref.shape
@@ -252,7 +250,6 @@
                 (rates_hbm, rates_ref),
                 (residues_hbm, residues_ref),
                 (direct_hbm, direct_ref),
-                (streams_hbm.at[0], stream_ref),
             )
         )
     ]
@@ -263,13 +260,7 @@
     sub = lax.broadcasted_iota(jnp.int32, (SUBS, LANES), 0)
     base = first + steps * sub
     for j in range(steps):
-        rows = slice(j * SUBS, (j + 1) * SUBS)
-        keep_scr[rows] = keep_rows(starts, base + j)
-        alive = jnp.ones((SUBS, LANES), F32)
-        for s in starts:
-            alive = jnp.where((s >= first) & (base + j >= s), 0.0, alive)
-        alive_scr[rows] = alive
-    keep_before = keep_rows(starts, base - 1)
+        keep_scr[j * SUBS : (j + 1) * SUBS] = keep_rows(starts, base + j)
     reach = chunk_reach(starts, first, steps)
     for c in copies:
         c.wait()
@@ -289,14 +280,10 @@
 
     def group(g, carry):
         lanes = pl.ds(pl.multiple_of(g * LANES, LANES), LANES)
-        for s in range(SUBS):
-            wide_scr[s * PITCH : s * PITCH + steps] = stream_ref[
-                s * steps : (s + 1) * steps, lanes
-            ].astype(F32)
+        decays = jnp.exp(-rates_ref[:, lanes])
         decay, weight, state = [], [], []
         for p in range(poles):
-            rate = jnp.broadcast_to(rates_ref[p : p + 1, lanes], (SUBS, LANES))
-            decay.append(jnp.exp(-rate))
+            decay.append(jnp.broadcast_to(decays[p : p + 1], (SUBS, LANES)))
             weight.append(jnp.broadcast_to(weight_scr[p : p + 1, lanes], (SUBS, LANES)))
             at = block_len + SUBS * (1 + p)
             total = chunk_ends(
@@ -314,9 +301,47 @@
                 driver = jnp.where(sub == 0, first_scr[j : j + 1, lanes], driver)
             keep = keep_scr[rows]
             state = [d * (keep * s) + driver for d, s in zip(decay, state)]
-            local_scr[rows] = summed(
+            local_ref[g, rows] = summed(
                 [w * s for w, s in zip(weight, state)] + [direct * driver]
             )
+        return carry
+
+    lax.fori_loop(0, chans // LANES, group, 0)
+
+
+def gate_kernel(
+    docs_ref, halo_ref, local_ref, streams_hbm, taps_hbm,
+    made_ref,
+    stream_ref, taps_ref, keep_scr, alive_scr, wide_scr, sems,
+):
+    block_len, chans = stream_ref.shape
+    steps = block_len // SUBS
+    copies = [
+        pltpu.make_async_copy(taps_hbm, taps_ref, sems.at[0]),
+        pltpu.make_async_copy(streams_hbm.at[0], stream_ref, sems.at[1]),
+    ]
+    for c in copies:
+        c.start()
+    first = lax.axis_index("seq") * block_len
+    starts = start_positions(docs_ref, docs_ref.shape[0])
+    base = first + steps * lax.broadcasted_iota(jnp.int32, (SUBS, LANES), 0)
+    for j in range(steps):
+        rows = slice(j * SUBS, (j + 1) * SUBS)
+        keep_scr[rows] = keep_rows(starts, base + j)
+        alive = jnp.ones((SUBS, LANES), F32)
+        for s in starts:
+            alive = jnp.where((s >= first) & (base + j >= s), 0.0, alive)
+        alive_scr[rows] = alive
+    keep_before = keep_rows(starts, base - 1)
+    for c in copies:
+        c.wait()
+
+    def group(g, carry):
+        lanes = pl.ds(pl.multiple_of(g * LANES, LANES), LANES)
+        for s in range(SUBS):
+            wide_scr[s * PITCH : s * PITCH + steps] = stream_ref[
+                s * steps : (s + 1) * steps, lanes
+            ].astype(F32)
         taps = [jnp.broadcast_to(taps_ref[0, n : n + 1, lanes], (SUBS, LANES)) for n in range(3)]
         queries = filter_steps(
             lambda j: wide_scr[pl.ds(j, SUBS, stride=PITCH), :],
@@ -329,7 +354,7 @@
         local, asked = [], []
         for j, query in enumerate(queries):
             rows = slice(j * SUBS, (j + 1) * SUBS)
-            local.append(query * local_scr[rows])
+            local.append(query * local_ref[g, rows])
             asked.append(query * alive_scr[rows])
             if j % 2 == 1:
                 rows = slice((j - 1) * SUBS, (j + 1) * SUBS)
@@ -349,11 +374,14 @@
 
 
 def out_kernel(
-    docs_ref, totals_ref, rates_ref, made_ref, unembed_hbm,
-    gated_hbm, logits_ref,
-    unembed_ref, gated_ref, arriving_scr, out_scr, sem, gated_sems,
-    *, block_len, row_members,
+    docs_ref, rates_ref, before_ref, made_ref, unembed_hbm, *totals_and_rest,
+    block_len, row_members, rows_back,
 ):
+    totals = totals_and_rest[:rows_back]
+    (
+        gated_hbm, logits_ref,
+        unembed_ref, gated_ref, arriving_scr, out_scr, sem, gated_sems,
+    ) = totals_and_rest[rows_back:]
     poles, chans = rates_ref.shape
     steps = block_len // SUBS
     groups = chans // LANES
@@ -370,17 +398,14 @@
     rates = rates_ref[...]
     row_transfer = jnp.exp(-rates * row_len)
     total = jnp.zeros(rates.shape, F32)
-    before = jnp.zeros(rates.shape, F32)
-    for j in range(totals_ref.shape[0]):
-        low = j * row_len
+    for back in range(rows_back, 0, -1):
+        low = (row - back) * row_len
         clean = no_start_in(starts, low, low + row_len)
-        arrived = totals_ref[j].astype(F32)
-        before = jnp.where(j == row, arrived, before)
-        total = jnp.where(j < row, (row_transfer * clean) * total + arrived, total)
+        total = (row_transfer * clean) * total + totals[back - 1][...].astype(F32)
     within = jnp.exp(-rates * (me * block_len).astype(F32)) * no_start_in(
         starts, row * row_len, first
     )
-    arriving_scr[...] = before + within * total
+    arriving_scr[...] = before_ref[...] + within * total
     sub = lax.broadcasted_iota(jnp.int32, (SUBS, LANES), 0)
 
     share = logits_ref.shape[1]
@@ -514,38 +539,23 @@
         name="joined_states",
     )(doc_lengths, halo, short_filter, pole_rates, residues, *kept_in_vmem(work))
     along_row = [[r * row_members + i for i in range(row_members)] for r in range(rows)]
-    across_rows = [[r * row_members + i for r in range(rows)] for i in range(row_members)]
     ends = lax.all_to_all(ends, "seq", 0, 0, axis_index_groups=along_row)
-    totals = pl.pallas_call(
-        functools.partial(row_kernel, block_len=block_len),
-        out_shape=pltpu.VMEM((rows, poles, chans), BF16),
-        in_specs=in_smem(1) + in_vmem(2),
-        out_specs=in_vmem(1)[0],
-        compiler_params=PARAMS,
-        name="row_states",
-    )(doc_lengths, pole_rates, ends)
-    totals, work, halo = lax.optimization_barrier((totals, work, halo))
-    totals = lax.all_to_all(totals, "seq", 0, 0, axis_index_groups=across_rows)
-    made = pl.pallas_call(
+    local_out = pl.pallas_call(
         functools.partial(local_kernel, block_len=block_len),
-        out_shape=pltpu.VMEM((2, block_len, chans), BF16),
-        in_specs=in_smem(1) + in_vmem(2) + in_hbm(5),
+        out_shape=pltpu.VMEM((groups, block_len, LANES), F32),
+        in_specs=in_smem(1) + in_vmem(2) + in_hbm(4),
         out_specs=in_vmem(1)[0],
         scratch_shapes=[
-            pltpu.VMEM((block_len, chans), BF16),
             pltpu.VMEM(short_filter.shape, F32),
             pltpu.VMEM(pole_rates.shape, F32),
             pltpu.VMEM(residues.shape, F32),
             pltpu.VMEM((1, chans), F32),
             pltpu.VMEM((block_len, LANES), F32),
-            pltpu.VMEM((block_len, LANES), F32),
             pltpu.VMEM((poles, chans), F32),
             pltpu.VMEM((poles, chans), F32),
             pltpu.VMEM((poles, chans), F32),
             pltpu.VMEM((2, chans), F32),
-            pltpu.VMEM((SUBS * PITCH, LANES), F32),
-            pltpu.VMEM((block_len, LANES), F32),
-            pltpu.SemaphoreType.DMA((5,)),
+            pltpu.SemaphoreType.DMA((4,)),
         ],
         compiler_params=PARAMS,
         cost_estimate=pl.CostEstimate(
@@ -554,15 +564,51 @@
         name="local_out",
     )(
         doc_lengths, halo, *kept_in_vmem(work),
-        *kept_in_hbm(streams, short_filter, pole_rates, residues, direct[None]),
+        *kept_in_hbm(short_filter, pole_rates, residues, direct[None]),
     )
+    ends, local_out = lax.optimization_barrier((ends, local_out))
+    total, before = pl.pallas_call(
+        functools.partial(row_kernel, block_len=block_len),
+        out_shape=(pltpu.VMEM((poles, chans), BF16), pltpu.VMEM((poles, chans), F32)),
+        in_specs=in_smem(1) + in_vmem(2),
+        out_specs=in_vmem(2),
+        compiler_params=PARAMS,
+        name="row_states",
+    )(doc_lengths, pole_rates, ends)
+    total, local_out, halo = lax.optimization_barrier((total, local_out, halo))
+    rows_back = min(rows - 1, -(-LONGEST // (block_len * row_members)))
+    totals = [
+        lax.ppermute(total, "seq", [(i, i + row_members * k) for i in range(seq - row_members * k)])
+        for k in range(1, rows_back + 1)
+    ]
+    made = pl.pallas_call(
+        gate_kernel,
+        out_shape=pltpu.VMEM((2, block_len, chans), BF16),
+        in_specs=in_smem(1) + in_vmem(2) + in_hbm(2),
+        out_specs=in_vmem(1)[0],
+        scratch_shapes=[
+            pltpu.VMEM((block_len, chans), BF16),
+            pltpu.VMEM(short_filter.shape, F32),
+            pltpu.VMEM((block_len, LANES), F32),
+            pltpu.VMEM((block_len, LANES), F32),
+            pltpu.VMEM((SUBS * PITCH, LANES), F32),
+            pltpu.SemaphoreType.DMA((2,)),
+        ],
+        compiler_params=PARAMS,
+        cost_estimate=pl.CostEstimate(
+            flops=50 * block_len * chans, bytes_accessed=4 * streams.size, transcendentals=0
+        ),
+        name="gated_local",
+    )(doc_lengths, halo, *kept_in_vmem(local_out), *kept_in_hbm(streams, short_filter))
     gated, logits = pl.pallas_call(
-        functools.partial(out_kernel, block_len=block_len, row_members=row_members),
+        functools.partial(
+            out_kernel, block_len=block_len, row_members=row_members, rows_back=rows_back
+        ),
         out_shape=(
             jax.ShapeDtypeStruct((block_len, chans), BF16),
             pltpu.VMEM((chan, share, vocab), BF16),
         ),
-        in_specs=in_smem(1) + in_vmem(3) + in_hbm(1),
+        in_specs=in_smem(1) + in_vmem(3) + in_hbm(1) + in_vmem(rows_back),
         out_specs=in_hbm(1) + in_vmem(1),
         scratch_shapes=[
             pltpu.VMEM(unembed.shape, BF16),
@@ -574,7 +620,7 @@
         ],
         compiler_params=PARAMS,
         name="gated_logits",
-    )(doc_lengths, totals, pole_rates, *kept_in_vmem(made), *kept_in_hbm(unembed))
+    )(doc_lengths, pole_rates, *kept_in_vmem(before, made), *kept_in_hbm(unembed), *totals)
     parts = lax.all_to_all(logits, "chan", 0, 0)
     losses = pl.pallas_call(
         loss_kernel,
@@ -590,7 +636,7 @@
 
 def solution(mesh):
     seq = mesh.shape["seq"]
-    row_members = 8 if seq % 8 == 0 else seq
+    row_members = 16 if seq % 16 == 0 else seq
     in_specs = (
         P(None, "seq", "chan"),
         P(None, None, "chan"),

time: 75.1 us -> 73.9 us (0.984)
  the two profiles are of different devices: /device:TPU:2 before, /device:TPU:16 now
where the time goes in v4:
time: 73.9 us; the launch traced here: 73.3 us
  blocking collectives  30.7 us (42%)
  Pallas kernels  16.5 us (22%)
  starting transfers between devices  13.8 us (19%)
  waiting for transfers between devices  10.1 us (14%)
  local copies, waits for them, and re-layouts  0.86 us (1%)
  between operations  0.78 us (1%)
    all_to_all x1, blocking collectives, local(): parts = lax.all_to_all(logits, 'chan', 0, 0)  20.6 us
    all_to_all x1, blocking collectives, local(): losses = lax.all_to_all(losses, 'chan', 0, 0)  10.1 us
    all_to_all x1, waiting for transfers between devices, local(): ends = lax.all_to_all(ends, 'seq', 0, 0, axis_index_groups=along_row)  6.11 us
    all_to_all x1, starting transfers between devices, local(): ends = lax.all_to_all(ends, 'seq', 0, 0, axis_index_groups=along_row)  6.03 us
    ppermute x2, starting transfers between devices, local(): lax.ppermute(total, 'seq', [(i, i + row_members * k) for i in range(seq -...  5.72 us
    pallas_call x1, Pallas kernels, local(): pl.pallas_call(functools.partial(local_kernel, block_len=block_len), out_...  4.74 us
    pallas_call x1, Pallas kernels, local(): pl.pallas_call(first_kernel, out_shape=pltpu.VMEM((groups, block_len + SU...  3.62 us
    pallas_call x1, Pallas kernels, local(): pl.pallas_call(functools.partial(out_kernel, block_len=block_len, row_mem...  2.71 us
  transfers between devices with their start and end apart: 4, of which 3 were waited for; matrix products, arithmetic and copies ran while one was open for 0% of the time, Pallas kernels for 15%

profile of v4, /device:TPU:16, one launch (start us, length us, event | category | flops | bytes accessed | tf_op | source)
XLA Modules:
  0.0 73.3 jit_solution(4861340749801412704)
XLA Ops:
  0.6 0.8 %slice.3 = bf16[3,2,1024]{2,1,0:T(2,128)(2,1)S(1)} slice(bf16[3,256,1024]{2,1,0:T(8,128)(2,1)} %streams_hbm.3), slice={[0:3], [254:256], [0:1024]} | slice | bytes 24576 | tf_op jit(solution)/shard_map/slice | solution.py:509
  1.4 0.0 copy-start
  1.5 0.0 copy-start.2
  1.5 0.0 copy-start.3
  1.5 0.0 copy-start.4
  1.5 2.1 %collective-permute-start = (bf16[3,2,1024]{2,1,0:T(2,128)(2,1)S(1)}, bf16[3,2,1024]{2,1,0:T(2,128)(2,1)S(1)}, u32[]{:S(2)}, u32[]{:S(2)}) collective-permute-start(bf16[3,2,1024]{2,1,0:T(2,128)(2,1)S(1)} %slice.3), channel_id=1, source_target_pairs={{0,8},{8,16},{16,24},{24,32},{32,40},{40,48},{48,56},{56,64},{64,7... | collective-permute-start | bytes 36872 | tf_op jit(solution)/shard_map/ppermute | solution.py:508
  3.6 3.6 %block_states.1.work_ref = f32[8,392,128]{2,1,0:T(8,128)S(1)} custom-call(s32[4]{0:T(128)} %docs_ref.9, bf16[3,256,1024]{2,1,0:T(8,128)(2,1)} %streams_hbm.3, f32[3,3,1024]{2,1,0:T(4,128)} %taps_hbm.5, f32[16,1024]{1,0:T(8,128)} %rates_ref.5), custom_call_target="tpu_custom_call" | custom-call | flops 15728640 | bytes 3145728 | tf_op jit(solution)/shard_map/block_states/pallas_call | solution.py:511
  7.2 1.6 %collective-permute-done.halo_ref = bf16[3,2,1024]{2,1,0:T(2,128)(2,1)S(1)} collective-permute-done((bf16[3,2,1024]{2,1,0:T(2,128)(2,1)S(1)}, bf16[3,2,1024]{2,1,0:T(2,128)(2,1)S(1)}, u32[]{:S(2)}, u32[]{:S(2)}) %collective-permute-start) | collective-permute-done | bytes 12320 | tf_op jit(solution)/shard_map/ppermute | solution.py:508
  8.8 0.0 copy-done
  8.8 0.0 copy-done.2
  8.8 0.0 copy-done.3
  8.8 0.0 copy-done.4
  8.8 1.6 %joined_states.1 = bf16[16,16,1024]{2,1,0:T(8,128)(2,1)} custom-call(s32[4]{0:T(128)S(1)} %copy-done.4, bf16[3,2,1024]{2,1,0:T(2,128)(2,1)S(1)} %collective-permute-done.halo_ref, f32[3,3,1024]{2,1,0:T(4,128)S(1)} %copy-done.2, f32[16,1024]{1,0:T(8,128)S(1)} %copy-done, f32[16,1024]{1,0:T(8,128)S(1)} %copy-done.3, f32[8,392,128]{2,1,0:T(8,128)S(1)} %block_states.1.work_ref), custom_call_target="tpu_custom_call" | custom-call | tf_op jit(solution)/shard_map/joined_states/pallas_call | solution.py:533
  10.4 6.0 %all-to-all-start = ((bf16[16,16,1024]{2,1,0:T(8,128)(2,1)}), bf16[16,16,1024]{2,1,0:T(8,128)(2,1)S(1)}, u32[]{:S(2)}, u32[]{:S(2)}) async-start(bf16[16,16,1024]{2,1,0:T(8,128)(2,1)} %joined_states.1), calls=%async_computation | async-start | bytes 1048576 | tf_op jit(solution)/shard_map/all_to_all | solution.py:542
  16.4 0.0 copy-start.1
  16.5 4.7 %local_out.1.local_ref = f32[8,256,128]{2,1,0:T(8,128)S(1)} custom-call(s32[4]{0:T(128)S(1)} %copy-done.4, bf16[3,2,1024]{2,1,0:T(2,128)(2,1)S(1)} %collective-permute-done.halo_ref, f32[8,392,128]{2,1,0:T(8,128)S(1)} %block_states.1.work_ref, f32[3,3,1024]{2,1,0:T(4,128)} %taps_hbm.5, f32[16,1024]{1,0:T(8,128)} %rates_ref.5, f32[16,1024]{1,0:T(8,128)} %residues_hbm.1, ...), custom_call_target="tpu_custom_call" | custom-call | flops 26214400 | bytes 6291456 | tf_op jit(solution)/shard_map/local_out/pallas_call | solution.py:543
  21.2 6.1 %all-to-all-done.ends_ref = bf16[16,16,1024]{2,1,0:T(8,128)(2,1)S(1)} async-done(((bf16[16,16,1024]{2,1,0:T(8,128)(2,1)}), bf16[16,16,1024]{2,1,0:T(8,128)(2,1)S(1)}, u32[]{:S(2)}, u32[]{:S(2)}) %all-to-all-start) | async-done | bytes 524320 | tf_op jit(solution)/shard_map/all_to_all | solution.py:542
  27.3 0.0 copy-done.1
  27.3 0.8 %row_states.1 = (bf16[16,1024]{1,0:T(8,128)(2,1)S(1)}, f32[16,1024]{1,0:T(8,128)S(1)}) custom-call(s32[4]{0:T(128)S(1)} %copy-done.4, f32[16,1024]{1,0:T(8,128)S(1)} %copy-done.1, bf16[16,16,1024]{2,1,0:T(8,128)(2,1)S(1)} %all-to-all-done.ends_ref), custom_call_target="tpu_custom_call" | custom-call | tf_op jit(solution)/shard_map/row_states/pallas_call | solution.py:570
  28.1 3.8 %collective-permute-start.2 = (bf16[16,1024]{1,0:T(8,128)(2,1)S(1)}, bf16[16,1024]{1,0:T(8,128)(2,1)S(1)}, u32[]{:S(2)}, u32[]{:S(2)}) collective-permute-start(bf16[16,1024]{1,0:T(8,128)(2,1)S(1)} %get-tuple-element.17), channel_id=1, source_target_pairs={{0,256},{8,264},{16,272},{24,280},{32,288},{40,296},{48,304},{56,3... | collective-permute-start | bytes 98312 | tf_op jit(solution)/shard_map/ppermute | solution.py:581
  31.9 1.9 %collective-permute-start.1 = (bf16[16,1024]{1,0:T(8,128)(2,1)S(1)}, bf16[16,1024]{1,0:T(8,128)(2,1)S(1)}, u32[]{:S(2)}, u32[]{:S(2)}) collective-permute-start(bf16[16,1024]{1,0:T(8,128)(2,1)S(1)} %get-tuple-element.17), channel_id=1, source_target_pairs={{0,128},{8,136},{16,144},{24,152},{32,160},{40,168},{48,176},{56,1... | collective-permute-start | bytes 98312 | tf_op jit(solution)/shard_map/ppermute | solution.py:581
  33.8 2.3 %gated_local.1.made_ref = bf16[2,256,1024]{2,1,0:T(8,128)(2,1)S(1)} custom-call(s32[4]{0:T(128)S(1)} %copy-done.4, bf16[3,2,1024]{2,1,0:T(2,128)(2,1)S(1)} %collective-permute-done.halo_ref, f32[8,256,128]{2,1,0:T(8,128)S(1)} %local_out.1.local_ref, bf16[3,256,1024]{2,1,0:T(8,128)(2,1)} %streams_hbm.3, f32[3,3,1024]{2,1,0:T(4,128)} %taps_hbm.5), custom_call_target="tpu_custom_call" | custom-call | flops 13107200 | bytes 3145728 | tf_op jit(solution)/shard_map/gated_local/pallas_call | solution.py:584
  36.1 0.0 copy-start.5
  36.2 0.0 collective-permute-done.2.totals_and_rest_1_
  36.2 2.4 %collective-permute-done.1.totals_and_rest_0_ = bf16[16,1024]{1,0:T(8,128)(2,1)S(1)} collective-permute-done((bf16[16,1024]{1,0:T(8,128)(2,1)S(1)}, bf16[16,1024]{1,0:T(8,128)(2,1)S(1)}, u32[]{:S(2)}, u32[]{:S(2)}) %collective-permute-start.1) | collective-permute-done | bytes 32800 | tf_op jit(solution)/shard_map/ppermute | solution.py:581
  38.6 2.7 %gated_logits.1 = (bf16[256,1024]{1,0:T(8,128)(2,1)}, bf16[8,32,512]{2,1,0:T(8,128)(2,1)S(1)}) custom-call(s32[4]{0:T(128)S(1)} %copy-done.4, f32[16,1024]{1,0:T(8,128)S(1)} %copy-done.1, f32[16,1024]{1,0:T(8,128)S(1)} %get-tuple-element.12.before_ref, bf16[2,256,1024]{2,1,0:T(8,128)(2,1)S(1)} %gated_local.1.made_ref, bf16[1024,512]{1,0:T(8,128)(2,1)} %unembed_hbm.1, ...), custom_call_target="tpu_custom_call" | custom-call | tf_op jit(solution)/shard_map/gated_logits/pallas_call | solution.py:603
  41.3 20.6 %all_to_all.15.parts_ref = bf16[8,32,512]{2,1,0:T(8,128)(2,1)S(1)} all-to-all(bf16[8,32,512]{2,1,0:T(8,128)(2,1)S(1)} %get-tuple-element.19), channel_id=1, replica_groups=mesh['seq'=64,'chan'=8] {'chan'}, dimensions={0} | all-to-all | bytes 524288 | tf_op jit(solution)/shard_map/all_to_all | solution.py:624
  61.9 0.0 copy-done.5
  61.9 0.8 %token_losses.1 = f32[8,2,128]{2,1,0:T(2,128)S(1)} custom-call(s32[256]{0:T(256)S(1)} %copy-done.5, bf16[8,32,512]{2,1,0:T(8,128)(2,1)S(1)} %all_to_all.15.parts_ref), custom_call_target="tpu_custom_call" | custom-call | tf_op jit(solution)/shard_map/token_losses/pallas_call | solution.py:625
  62.7 10.1 %all_to_all.16 = f32[8,2,128]{2,1,0:T(2,128)S(1)} all-to-all(f32[8,2,128]{2,1,0:T(2,128)S(1)} %token_losses.1), channel_id=1, replica_groups=mesh['seq'=64,'chan'=8] {'chan'}, dimensions={0} | all-to-all | bytes 16384 | tf_op jit(solution)/shard_map/all_to_all | solution.py:633
  72.8 0.6 reduce_sum.9
Async XLA Ops:
  1.4 7.3 %copy-start = (f32[16,1024]{1,0:T(8,128)S(1)}, f32[16,1024]{1,0:T(8,128)}, u32[]{:S(2)}) copy-start(f32[16,1024]{1,0:T(8,128)} %rates_ref.5) | copy-start | bytes 196612
  1.5 7.3 %copy-start.2 = (f32[3,3,1024]{2,1,0:T(4,128)S(1)}, f32[3,3,1024]{2,1,0:T(4,128)}, u32[]{:S(2)}) copy-start(f32[3,3,1024]{2,1,0:T(4,128)} %taps_hbm.5) | copy-start | bytes 110596
  1.5 7.3 %copy-start.3 = (f32[16,1024]{1,0:T(8,128)S(1)}, f32[16,1024]{1,0:T(8,128)}, u32[]{:S(2)}) copy-start(f32[16,1024]{1,0:T(8,128)} %residues_hbm.1) | copy-start | bytes 196612
  1.5 7.3 %copy-start.4 = (s32[4]{0:T(128)S(1)}, s32[4]{0:T(128)}, u32[]{:S(2)}) copy-start(s32[4]{0:T(128)} %docs_ref.9) | copy-start | bytes 52
  1.5 7.3 %collective-permute-start = (bf16[3,2,1024]{2,1,0:T(2,128)(2,1)S(1)}, bf16[3,2,1024]{2,1,0:T(2,128)(2,1)S(1)}, u32[]{:S(2)}, u32[]{:S(2)}) collective-permute-start(bf16[3,2,1024]{2,1,0:T(2,128)(2,1)S(1)} %slice.3), channel_id=1, source_target_pairs={{0,8},{8,16},{16,24},{24,32},{32,40},{40,48},{48,56},{56,64},{64,7... | collective-permute-start | bytes 36872 | tf_op jit(solution)/shard_map/ppermute | solution.py:508
  10.4 16.9 %all-to-all-start = ((bf16[16,16,1024]{2,1,0:T(8,128)(2,1)}), bf16[16,16,1024]{2,1,0:T(8,128)(2,1)S(1)}, u32[]{:S(2)}, u32[]{:S(2)}) async-start(bf16[16,16,1024]{2,1,0:T(8,128)(2,1)} %joined_states.1), calls=%async_computation | async-start | bytes 1048576 | tf_op jit(solution)/shard_map/all_to_all | solution.py:542
  16.4 10.9 %copy-start.1 = (f32[16,1024]{1,0:T(8,128)S(1)}, f32[16,1024]{1,0:T(8,128)}, u32[]{:S(2)}) copy-start(f32[16,1024]{1,0:T(8,128)} %rates_ref.5) | copy-start | bytes 196612
  28.1 8.1 %collective-permute-start.2 = (bf16[16,1024]{1,0:T(8,128)(2,1)S(1)}, bf16[16,1024]{1,0:T(8,128)(2,1)S(1)}, u32[]{:S(2)}, u32[]{:S(2)}) collective-permute-start(bf16[16,1024]{1,0:T(8,128)(2,1)S(1)} %get-tuple-element.17), channel_id=1, source_target_pairs={{0,256},{8,264},{16,272},{24,280},{32,288},{40,296},{48,304},{56,3... | collective-permute-start | bytes 98312 | tf_op jit(solution)/shard_map/ppermute | solution.py:581
  31.9 6.7 %collective-permute-start.1 = (bf16[16,1024]{1,0:T(8,128)(2,1)S(1)}, bf16[16,1024]{1,0:T(8,128)(2,1)S(1)}, u32[]{:S(2)}, u32[]{:S(2)}) collective-permute-start(bf16[16,1024]{1,0:T(8,128)(2,1)S(1)} %get-tuple-element.17), channel_id=1, source_target_pairs={{0,128},{8,136},{16,144},{24,152},{32,160},{40,168},{48,176},{56,1... | collective-permute-start | bytes 98312 | tf_op jit(solution)/shard_map/ppermute | solution.py:581
  36.1 25.8 %copy-start.5 = (s32[256]{0:T(256)S(1)}, s32[256]{0:T(256)}, u32[]{:S(2)}) copy-start(s32[256]{0:T(256)} %targets_ref.1) | copy-start | bytes 3076

commit v5 on v4

--- a/solution.py
+++ b/solution.py
@@ -117,10 +117,8 @@
                 steps,
             )
 
-        decay = [
-            jnp.broadcast_to(jnp.exp(-rates_ref[p : p + 1, lanes]), (SUBS, LANES))
-            for p in range(poles)
-        ]
+        decays = jnp.exp(-rates_ref[:, lanes])
+        decay = [jnp.broadcast_to(decays[p : p + 1], (SUBS, LANES)) for p in range(poles)]
         state = [jnp.zeros((SUBS, LANES), F32) for _ in range(poles)]
         for j, (key, value) in enumerate(zip(steps_of(0), steps_of(1))):
             rows = slice(j * SUBS, (j + 1) * SUBS)
@@ -455,18 +453,16 @@
         logits = logits + parts_ref[i].astype(F32)
     place = lax.axis_index("chan")
     first = place * share
-    row = lax.broadcasted_iota(jnp.int32, (share, 1), 0)
-    target = jnp.zeros((share, 1), jnp.int32)
-    for t in range(share):
-        target = jnp.where(row == t, targets_ref[first + t], target)
+    lines, wide = loss_ref.shape[1:]
+    lane = lax.broadcasted_iota(jnp.int32, (share, wide), 1)
+    mine = lane == lax.rem(first, wide) + lax.broadcasted_iota(jnp.int32, (share, wide), 0)
+    near = targets_ref[pl.ds(lax.div(first, wide), 1), :].astype(F32)
+    target = jnp.sum(jnp.where(mine, near, 0.0), axis=1, keepdims=True).astype(jnp.int32)
     peak = jnp.max(logits, axis=1, keepdims=True)
     total = jnp.sum(jnp.exp(logits - peak), axis=1, keepdims=True)
     ids = lax.broadcasted_iota(jnp.int32, logits.shape, 1)
     picked = jnp.sum(jnp.where(ids == target, logits, 0.0), axis=1, keepdims=True)
     loss = peak + jnp.log(total) - picked
-    lines, wide = loss_ref.shape[1:]
-    lane = lax.broadcasted_iota(jnp.int32, (share, wide), 1)
-    mine = lane == lax.rem(first, wide) + lax.broadcasted_iota(jnp.int32, (share, wide), 0)
     line = jnp.sum(jnp.where(mine, loss, 0.0), axis=0, keepdims=True)
     at = lax.broadcasted_iota(jnp.int32, (lines, wide), 0) == lax.div(first, wide)
     placed = jnp.where(at, line, 0.0)
@@ -625,11 +621,11 @@
     losses = pl.pallas_call(
         loss_kernel,
         out_shape=pltpu.VMEM((chan, block_len // LANES, LANES), F32),
-        in_specs=in_smem(1) + in_vmem(1),
+        in_specs=in_vmem(2),
         out_specs=pl.BlockSpec(memory_space=pltpu.VMEM),
         compiler_params=PARAMS,
         name="token_losses",
-    )(targets, parts)
+    )(targets.reshape(block_len // LANES, LANES), parts)
     losses = lax.all_to_all(losses, "chan", 0, 0)
     return gated, jnp.sum(losses, axis=0).reshape(block_len)
 

time: 73.9 us -> 73.3 us (level)
  no operation moved by 1% of the time
where the time goes in v5:
time: 73.3 us; the launch traced here: 72.8 us
  blocking collectives  30.7 us (42%)
  Pallas kernels  16 us (22%)
  starting transfers between devices  13.8 us (19%)
  waiting for transfers between devices  10.1 us (14%)
  local copies, waits for them, and re-layouts  0.86 us (1%)
  between operations  0.78 us (1%)
    all_to_all x1, blocking collectives, local(): parts = lax.all_to_all(logits, 'chan', 0, 0)  20.6 us
    all_to_all x1, blocking collectives, local(): losses = lax.all_to_all(losses, 'chan', 0, 0)  10.1 us
    all_to_all x1, waiting for transfers between devices, local(): ends = lax.all_to_all(ends, 'seq', 0, 0, axis_index_groups=along_row)  6.11 us
    all_to_all x1, starting transfers between devices, local(): ends = lax.all_to_all(ends, 'seq', 0, 0, axis_index_groups=along_row)  5.99 us
    ppermute x2, starting transfers between devices, local(): lax.ppermute(total, 'seq', [(i, i + row_members * k) for i in range(seq -...  5.75 us
    pallas_call x1, Pallas kernels, local(): pl.pallas_call(functools.partial(local_kernel, block_len=block_len), out_...  4.74 us
    pallas_call x1, Pallas kernels, local(): pl.pallas_call(first_kernel, out_shape=pltpu.VMEM((groups, block_len + SU...  3.59 us
    pallas_call x1, Pallas kernels, local(): pl.pallas_call(functools.partial(out_kernel, block_len=block_len, row_mem...  2.71 us
  transfers between devices with their start and end apart: 4, of which 3 were waited for; matrix products, arithmetic and copies ran while one was open for 0% of the time, Pallas kernels for 15%

profile of v5, /device:TPU:16, one launch (start us, length us, event | category | flops | bytes accessed | tf_op | source)
XLA Modules:
  0.0 72.8 jit_solution(12205723982329074862)
XLA Ops:
  0.6 0.8 %slice.3 = bf16[3,2,1024]{2,1,0:T(2,128)(2,1)S(1)} slice(bf16[3,256,1024]{2,1,0:T(8,128)(2,1)} %streams_hbm.3), slice={[0:3], [254:256], [0:1024]} | slice | bytes 24576 | tf_op jit(solution)/shard_map/slice | solution.py:505
  1.4 0.0 copy-start
  1.5 0.0 copy-start.2
  1.5 0.0 copy-start.3
  1.5 0.0 copy-start.4
  1.5 2.1 %collective-permute-start = (bf16[3,2,1024]{2,1,0:T(2,128)(2,1)S(1)}, bf16[3,2,1024]{2,1,0:T(2,128)(2,1)S(1)}, u32[]{:S(2)}, u32[]{:S(2)}) collective-permute-start(bf16[3,2,1024]{2,1,0:T(2,128)(2,1)S(1)} %slice.3), channel_id=1, source_target_pairs={{0,8},{8,16},{16,24},{24,32},{32,40},{40,48},{48,56},{56,64},{64,7... | collective-permute-start | bytes 36872 | tf_op jit(solution)/shard_map/ppermute | solution.py:504
  3.6 3.6 %block_states.1.work_ref = f32[8,392,128]{2,1,0:T(8,128)S(1)} custom-call(s32[4]{0:T(128)} %docs_ref.9, bf16[3,256,1024]{2,1,0:T(8,128)(2,1)} %streams_hbm.3, f32[3,3,1024]{2,1,0:T(4,128)} %taps_hbm.5, f32[16,1024]{1,0:T(8,128)} %rates_ref.5), custom_call_target="tpu_custom_call" | custom-call | flops 15728640 | bytes 3145728 | tf_op jit(solution)/shard_map/block_states/pallas_call | solution.py:507
  7.2 1.6 %collective-permute-done.halo_ref = bf16[3,2,1024]{2,1,0:T(2,128)(2,1)S(1)} collective-permute-done((bf16[3,2,1024]{2,1,0:T(2,128)(2,1)S(1)}, bf16[3,2,1024]{2,1,0:T(2,128)(2,1)S(1)}, u32[]{:S(2)}, u32[]{:S(2)}) %collective-permute-start) | collective-permute-done | bytes 12320 | tf_op jit(solution)/shard_map/ppermute | solution.py:504
  8.8 0.0 copy-done
  8.8 0.0 copy-done.2
  8.8 0.0 copy-done.3
  8.8 0.0 copy-done.4
  8.8 1.6 %joined_states.1 = bf16[16,16,1024]{2,1,0:T(8,128)(2,1)} custom-call(s32[4]{0:T(128)S(1)} %copy-done.4, bf16[3,2,1024]{2,1,0:T(2,128)(2,1)S(1)} %collective-permute-done.halo_ref, f32[3,3,1024]{2,1,0:T(4,128)S(1)} %copy-done.2, f32[16,1024]{1,0:T(8,128)S(1)} %copy-done, f32[16,1024]{1,0:T(8,128)S(1)} %copy-done.3, f32[8,392,128]{2,1,0:T(8,128)S(1)} %block_states.1.work_ref), custom_call_target="tpu_custom_call" | custom-call | tf_op jit(solution)/shard_map/joined_states/pallas_call | solution.py:529
  10.4 6.0 %all-to-all-start = ((bf16[16,16,1024]{2,1,0:T(8,128)(2,1)}), bf16[16,16,1024]{2,1,0:T(8,128)(2,1)S(1)}, u32[]{:S(2)}, u32[]{:S(2)}) async-start(bf16[16,16,1024]{2,1,0:T(8,128)(2,1)} %joined_states.1), calls=%async_computation | async-start | bytes 1048576 | tf_op jit(solution)/shard_map/all_to_all | solution.py:538
  16.4 0.0 copy-start.1
  16.4 4.7 %local_out.1.local_ref = f32[8,256,128]{2,1,0:T(8,128)S(1)} custom-call(s32[4]{0:T(128)S(1)} %copy-done.4, bf16[3,2,1024]{2,1,0:T(2,128)(2,1)S(1)} %collective-permute-done.halo_ref, f32[8,392,128]{2,1,0:T(8,128)S(1)} %block_states.1.work_ref, f32[3,3,1024]{2,1,0:T(4,128)} %taps_hbm.5, f32[16,1024]{1,0:T(8,128)} %rates_ref.5, f32[16,1024]{1,0:T(8,128)} %residues_hbm.1, ...), custom_call_target="tpu_custom_call" | custom-call | flops 26214400 | bytes 6291456 | tf_op jit(solution)/shard_map/local_out/pallas_call | solution.py:539
  21.2 6.1 %all-to-all-done.ends_ref = bf16[16,16,1024]{2,1,0:T(8,128)(2,1)S(1)} async-done(((bf16[16,16,1024]{2,1,0:T(8,128)(2,1)}), bf16[16,16,1024]{2,1,0:T(8,128)(2,1)S(1)}, u32[]{:S(2)}, u32[]{:S(2)}) %all-to-all-start) | async-done | bytes 524320 | tf_op jit(solution)/shard_map/all_to_all | solution.py:538
  27.3 0.0 copy-done.1
  27.3 0.8 %row_states.1 = (bf16[16,1024]{1,0:T(8,128)(2,1)S(1)}, f32[16,1024]{1,0:T(8,128)S(1)}) custom-call(s32[4]{0:T(128)S(1)} %copy-done.4, f32[16,1024]{1,0:T(8,128)S(1)} %copy-done.1, bf16[16,16,1024]{2,1,0:T(8,128)(2,1)S(1)} %all-to-all-done.ends_ref), custom_call_target="tpu_custom_call" | custom-call | tf_op jit(solution)/shard_map/row_states/pallas_call | solution.py:566
  28.1 3.8 %collective-permute-start.2 = (bf16[16,1024]{1,0:T(8,128)(2,1)S(1)}, bf16[16,1024]{1,0:T(8,128)(2,1)S(1)}, u32[]{:S(2)}, u32[]{:S(2)}) collective-permute-start(bf16[16,1024]{1,0:T(8,128)(2,1)S(1)} %get-tuple-element.17), channel_id=1, source_target_pairs={{0,256},{8,264},{16,272},{24,280},{32,288},{40,296},{48,304},{56,3... | collective-permute-start | bytes 98312 | tf_op jit(solution)/shard_map/ppermute | solution.py:577
  31.9 2.0 %collective-permute-start.1 = (bf16[16,1024]{1,0:T(8,128)(2,1)S(1)}, bf16[16,1024]{1,0:T(8,128)(2,1)S(1)}, u32[]{:S(2)}, u32[]{:S(2)}) collective-permute-start(bf16[16,1024]{1,0:T(8,128)(2,1)S(1)} %get-tuple-element.17), channel_id=1, source_target_pairs={{0,128},{8,136},{16,144},{24,152},{32,160},{40,168},{48,176},{56,1... | collective-permute-start | bytes 98312 | tf_op jit(solution)/shard_map/ppermute | solution.py:577
  33.8 2.3 %gated_local.1.made_ref = bf16[2,256,1024]{2,1,0:T(8,128)(2,1)S(1)} custom-call(s32[4]{0:T(128)S(1)} %copy-done.4, bf16[3,2,1024]{2,1,0:T(2,128)(2,1)S(1)} %collective-permute-done.halo_ref, f32[8,256,128]{2,1,0:T(8,128)S(1)} %local_out.1.local_ref, bf16[3,256,1024]{2,1,0:T(8,128)(2,1)} %streams_hbm.3, f32[3,3,1024]{2,1,0:T(4,128)} %taps_hbm.5), custom_call_target="tpu_custom_call" | custom-call | flops 13107200 | bytes 3145728 | tf_op jit(solution)/shard_map/gated_local/pallas_call | solution.py:580
  36.1 0.0 copy-start.5
  36.2 0.0 collective-permute-done.2.totals_and_rest_1_
  36.2 2.4 %collective-permute-done.1.totals_and_rest_0_ = bf16[16,1024]{1,0:T(8,128)(2,1)S(1)} collective-permute-done((bf16[16,1024]{1,0:T(8,128)(2,1)S(1)}, bf16[16,1024]{1,0:T(8,128)(2,1)S(1)}, u32[]{:S(2)}, u32[]{:S(2)}) %collective-permute-start.1) | collective-permute-done | bytes 32800 | tf_op jit(solution)/shard_map/ppermute | solution.py:577
  38.6 2.7 %gated_logits.1 = (bf16[256,1024]{1,0:T(8,128)(2,1)}, bf16[8,32,512]{2,1,0:T(8,128)(2,1)S(1)}) custom-call(s32[4]{0:T(128)S(1)} %copy-done.4, f32[16,1024]{1,0:T(8,128)S(1)} %copy-done.1, f32[16,1024]{1,0:T(8,128)S(1)} %get-tuple-element.12.before_ref, bf16[2,256,1024]{2,1,0:T(8,128)(2,1)S(1)} %gated_local.1.made_ref, bf16[1024,512]{1,0:T(8,128)(2,1)} %unembed_hbm.1, ...), custom_call_target="tpu_custom_call" | custom-call | tf_op jit(solution)/shard_map/gated_logits/pallas_call | solution.py:599
  41.3 20.6 %all_to_all.15.parts_ref = bf16[8,32,512]{2,1,0:T(8,128)(2,1)S(1)} all-to-all(bf16[8,32,512]{2,1,0:T(8,128)(2,1)S(1)} %get-tuple-element.19), channel_id=1, replica_groups=mesh['seq'=64,'chan'=8] {'chan'}, dimensions={0} | all-to-all | bytes 524288 | tf_op jit(solution)/shard_map/all_to_all | solution.py:620
  61.9 0.0 copy-done.5
  61.9 0.2 token_losses.1
  62.1 10.1 %all_to_all.16 = f32[8,2,128]{2,1,0:T(2,128)S(1)} all-to-all(f32[8,2,128]{2,1,0:T(2,128)S(1)} %token_losses.1), channel_id=1, replica_groups=mesh['seq'=64,'chan'=8] {'chan'}, dimensions={0} | all-to-all | bytes 16384 | tf_op jit(solution)/shard_map/all_to_all | solution.py:629
  72.2 0.6 reduce_sum.9
Async XLA Ops:
  1.4 7.3 %copy-start = (f32[16,1024]{1,0:T(8,128)S(1)}, f32[16,1024]{1,0:T(8,128)}, u32[]{:S(2)}) copy-start(f32[16,1024]{1,0:T(8,128)} %rates_ref.5) | copy-start | bytes 196612
  1.5 7.3 %copy-start.2 = (f32[3,3,1024]{2,1,0:T(4,128)S(1)}, f32[3,3,1024]{2,1,0:T(4,128)}, u32[]{:S(2)}) copy-start(f32[3,3,1024]{2,1,0:T(4,128)} %taps_hbm.5) | copy-start | bytes 110596
  1.5 7.3 %copy-start.3 = (f32[16,1024]{1,0:T(8,128)S(1)}, f32[16,1024]{1,0:T(8,128)}, u32[]{:S(2)}) copy-start(f32[16,1024]{1,0:T(8,128)} %residues_hbm.1) | copy-start | bytes 196612
  1.5 7.3 %copy-start.4 = (s32[4]{0:T(128)S(1)}, s32[4]{0:T(128)}, u32[]{:S(2)}) copy-start(s32[4]{0:T(128)} %docs_ref.9) | copy-start | bytes 52
  1.5 7.3 %collective-permute-start = (bf16[3,2,1024]{2,1,0:T(2,128)(2,1)S(1)}, bf16[3,2,1024]{2,1,0:T(2,128)(2,1)S(1)}, u32[]{:S(2)}, u32[]{:S(2)}) collective-permute-start(bf16[3,2,1024]{2,1,0:T(2,128)(2,1)S(1)} %slice.3), channel_id=1, source_target_pairs={{0,8},{8,16},{16,24},{24,32},{32,40},{40,48},{48,56},{56,64},{64,7... | collective-permute-start | bytes 36872 | tf_op jit(solution)/shard_map/ppermute | solution.py:504
  10.4 16.9 %all-to-all-start = ((bf16[16,16,1024]{2,1,0:T(8,128)(2,1)}), bf16[16,16,1024]{2,1,0:T(8,128)(2,1)S(1)}, u32[]{:S(2)}, u32[]{:S(2)}) async-start(bf16[16,16,1024]{2,1,0:T(8,128)(2,1)} %joined_states.1), calls=%async_computation | async-start | bytes 1048576 | tf_op jit(solution)/shard_map/all_to_all | solution.py:538
  16.4 10.9 %copy-start.1 = (f32[16,1024]{1,0:T(8,128)S(1)}, f32[16,1024]{1,0:T(8,128)}, u32[]{:S(2)}) copy-start(f32[16,1024]{1,0:T(8,128)} %rates_ref.5) | copy-start | bytes 196612
  28.1 8.1 %collective-permute-start.2 = (bf16[16,1024]{1,0:T(8,128)(2,1)S(1)}, bf16[16,1024]{1,0:T(8,128)(2,1)S(1)}, u32[]{:S(2)}, u32[]{:S(2)}) collective-permute-start(bf16[16,1024]{1,0:T(8,128)(2,1)S(1)} %get-tuple-element.17), channel_id=1, source_target_pairs={{0,256},{8,264},{16,272},{24,280},{32,288},{40,296},{48,304},{56,3... | collective-permute-start | bytes 98312 | tf_op jit(solution)/shard_map/ppermute | solution.py:577
  31.9 6.7 %collective-permute-start.1 = (bf16[16,1024]{1,0:T(8,128)(2,1)S(1)}, bf16[16,1024]{1,0:T(8,128)(2,1)S(1)}, u32[]{:S(2)}, u32[]{:S(2)}) collective-permute-start(bf16[16,1024]{1,0:T(8,128)(2,1)S(1)} %get-tuple-element.17), channel_id=1, source_target_pairs={{0,128},{8,136},{16,144},{24,152},{32,160},{40,168},{48,176},{56,1... | collective-permute-start | bytes 98312 | tf_op jit(solution)/shard_map/ppermute | solution.py:577
  36.1 25.7 %copy-start.5 = (s32[256]{0:T(256)S(1)}, s32[256]{0:T(256)}, u32[]{:S(2)}) copy-start(s32[256]{0:T(256)} %param.14) | copy-start | bytes 3076
